TPU v7x, 768 devices: a whole 4x8x12 slice. The times are simulated.
768 devices in a mesh: blk: 48 (over y_hi, z), group: 16 (over y_lo, x, core).
Axes of the slice: x: 4, y: 8 (y_hi: 4, y_lo: 2; y = y_hi * 2 + y_lo), z: 12, core: 2. Of those that a mesh axis runs over, the one named last changes fastest.
Arguments:
- image_emb: bfloat16 [98304, 1152], P(('blk', 'group')), may hold values from -0.1875 to 0.1875
- text_feats: bfloat16 [98304, 1152], P(('blk', 'group')), may hold values from -0.75 to 0.75
- text_head: bfloat16 [1152, 1152], replicated, may hold values from -0.1875 to 0.1875
- scale_logarithm: float32 [1], replicated, may hold values from 1.6 to 2.6
- logit_bias: float32 [1], replicated, may hold values from -5 to -2
- pair_index: int32 [98304], P(('blk', 'group')), may hold values from 0 to 98303, as said below
Outputs:
- image_grad: float32 [98304, 1152], P(('blk', 'group'))
- text_grad: float32 [98304, 1152], P(('blk', 'group'))
- head_grad: float32 [1152, 1152], P('blk', 'group')
- row_loss: float32 [98304], P(('blk', 'group'))
Inputs may be any that keep to these rules, and one draw needn't show every extreme that they name: `pair_index`: row r's pair id is r, or for some rows (r + 128), (r + 16 * 128) or (r + (16 + 1) * 128) modulo 98304.
All inputs are finite; a program needn't handle non-finite values.
Results may differ from a plain program's by a relative error of at most 0.022.
Values may be sent and summed in bfloat16 or wider, within the bound.
No kernel may reach another device: no remote copies, remote signals or barrier semaphores. Data moves between devices by JAX's collectives and lax.ppermute only.
A program may use at most 32 MiB of HBM per device.

v0:
```python
import jax
import jax.numpy as jnp
from jax import lax
from jax.sharding import PartitionSpec as P

HOPS = 2


EPS = 1e-06


def for_sending(value):

    def short(part):
        return part.astype(jnp.bfloat16) if part.dtype == jnp.float32 else part

    return jax.tree.map(short, value)


def shifted(value, axis, by):
    length = lax.axis_size(axis)
    return lax.ppermute(value, axis, [(i, (i + by) % length) for i in range(length)])


def unit_rows(vectors):
    lengths = jnp.sqrt(jnp.sum(vectors * vectors, axis=-1, keepdims=True) + EPS)
    return (vectors / lengths, lengths)


def score_block(
    left_operand, left_pair_index, right_operand, right_pair_index, scale_factor, logit_shift_bias
):
    unscaled_score = lax.dot_general(
        left_operand, right_operand, (((1,), (1,)), ((), ())), preferred_element_type=jnp.float32
    )
    logit_matrix = scale_factor * unscaled_score + logit_shift_bias
    target = jnp.where(left_pair_index[:, None] == right_pair_index[None, :], 1.0, -1.0).astype(
        jnp.float32
    )
    row_loss = jnp.sum(jax.nn.softplus(-target * logit_matrix), axis=1)
    logit_gradient = (-target * jax.nn.sigmoid(-target * logit_matrix)).astype(jnp.bfloat16)
    return (row_loss, logit_gradient)


def left_matmul(logit_gradient, left_operand):
    return lax.dot_general(
        logit_gradient, left_operand, (((0,), (0,)), ((), ())), preferred_element_type=jnp.float32
    )


def move_rows(payload, axis_name, amount):
    if axis_name == "blk":
        return jax.tree.map(
            lambda part, own: part.astype(own.dtype),
            shifted(for_sending(payload), "blk", amount),
            payload,
        )
    return jax.tree.map(
        lambda part, own: part.astype(own.dtype),
        shifted(for_sending(payload), "group", amount),
        payload,
    )


def move_grads(payload, axis_name, amount):
    if axis_name == "blk":
        return shifted(payload, "blk", amount)
    return shifted(payload, "group", amount)


def journey():
    moves_list = []
    for hop_idx in range(HOPS):
        moves_list.append(("blk", 1 if hop_idx % 2 == 0 else -1))
        if hop_idx < HOPS - 1:
            moves_list.append(("group", 1))
    return moves_list


def body(image_emb, text_feats, text_head, scale_logarithm, logit_bias, pair_index):
    scale_factor = jnp.exp(scale_logarithm[0])
    logit_shift_bias = logit_bias[0]
    image_unit, image_len = unit_rows(image_emb.astype(jnp.float32))
    image_halfwide = image_unit.astype(jnp.bfloat16)
    text_pre = jnp.dot(text_feats, text_head, preferred_element_type=jnp.float32)
    text_unit, text_len = unit_rows(text_pre)
    text_bf = text_unit.astype(jnp.bfloat16)
    moves_list = journey()
    sections = len(moves_list) + 1
    image_gradient = jnp.zeros(image_unit.shape, jnp.float32)
    loss_total = jnp.zeros((image_unit.shape[0],), jnp.float32)
    visiting_block = (text_bf, pair_index)
    carried_over = jnp.zeros(text_unit.shape, jnp.float32)
    for section in range(sections):
        row_loss, logit_gradient = score_block(
            image_halfwide,
            pair_index,
            visiting_block[0],
            visiting_block[1],
            scale_factor,
            logit_shift_bias,
        )
        loss_total = loss_total + row_loss
        image_gradient = image_gradient + scale_factor * jnp.dot(
            logit_gradient, visiting_block[0], preferred_element_type=jnp.float32
        )
        carried_over = carried_over + scale_factor * left_matmul(logit_gradient, image_halfwide)
        if section < len(moves_list):
            axis_name, amount = moves_list[section]
            visiting_block = move_rows(visiting_block, axis_name, amount)
            carried_over = move_grads(carried_over, axis_name, amount)
    group_back = sum([amount for axis_name, amount in moves_list if axis_name == "group"])
    carried_over = move_grads(carried_over, "group", -group_back)
    image_grad = (
        image_gradient - image_unit * jnp.sum(image_unit * image_gradient, axis=-1, keepdims=True)
    ) / image_len
    text_delta = (
        (carried_over - text_unit * jnp.sum(text_unit * carried_over, axis=-1, keepdims=True))
        / text_len
    ).astype(jnp.bfloat16)
    text_grad = lax.dot_general(
        text_delta, text_head, (((1,), (1,)), ((), ())), preferred_element_type=jnp.float32
    )
    head_term = lax.dot_general(
        text_feats, text_delta, (((0,), (0,)), ((), ())), preferred_element_type=jnp.float32
    )
    column_sums = lax.psum_scatter(
        head_term.astype(jnp.bfloat16), "group", scatter_dimension=1, tiled=True
    ).astype(jnp.float32)
    head_grad = lax.psum_scatter(column_sums, "blk", scatter_dimension=0, tiled=True)
    return (image_grad, text_grad, head_grad, loss_total)


def solution(mesh):
    placed = (
        P(("blk", "group"), None),
        P(("blk", "group"), None),
        P(),
        P(),
        P(),
        P(("blk", "group")),
    )
    return jax.shard_map(
        body,
        mesh=mesh,
        in_specs=placed,
        out_specs=(
            P(("blk", "group"), None),
            P(("blk", "group"), None),
            P("blk", "group"),
            P(("blk", "group")),
        ),
        check_vma=False,
    )
```

profile of v0, /device:TPU:8, one launch (start us, length us, event | category | flops | bytes accessed | tf_op | source)
XLA Modules:
  0.0 455.3 jit_solution(17263836400189876730)
XLA Ops:
  7.2 0.0 copy-start
  7.2 0.0 reduce-scatter.6.cloned.1.call-start
  8.7 0.0 copy-start.14
  8.7 1.1 fusion.11
  9.8 1.1 fusion.19
  10.9 0.0 copy-done
  10.9 1.6 multiply_reduce_fusion.2
  12.6 0.0 copy-start.15
  12.6 0.1 fusion.20
  12.7 0.0 copy-start.2
  12.8 0.8 fusion.12
  13.6 0.3 convolution_multiply_fusion.3
  13.9 4.3 collective-permute-start.6
  18.2 4.3 collective-permute-start.1
  22.5 4.3 collective-permute-start
  26.7 41.7 %collective-permute-done = s32[128]{0:T(128)S(1)} collective-permute-done((s32[128]{0:T(128)S(1)}, s32[128]{0:T(128)S(1)}, u32[]{:S(2)}, u32[]{:S(2)}) %collective-permute-start) | collective-permute-done | bytes 544 | tf_op jit(solution)/shard_map/ppermute | solution.py:22
  68.4 0.0 collective-permute-done.1
  68.5 0.9 fusion.13
  69.3 0.0 collective-permute-done.6
  69.3 0.6 copy-done.10
  69.9 0.3 fusion.1
  70.2 1.9 collective-permute-start.7
  72.1 3.5 collective-permute-start.3
  75.7 1.9 collective-permute-start.2
  77.6 9.2 %collective-permute-done.2 = s32[128]{0:T(128)S(1)} collective-permute-done((s32[128]{0:T(128)S(1)}, s32[128]{0:T(128)S(1)}, u32[]{:S(2)}, u32[]{:S(2)}) %collective-permute-start.2) | collective-permute-done | bytes 544 | tf_op jit(solution)/shard_map/ppermute | solution.py:22
  86.7 0.0 collective-permute-done.3
  86.8 0.8 fusion.14
  87.6 0.0 collective-permute-done.7
  87.6 0.3 fusion.17
  87.9 0.0 copy-done.2
  87.9 1.9 collective-permute-start.8
  89.8 1.9 collective-permute-start.5
  91.7 1.9 collective-permute-start.4
  93.7 29.1 %collective-permute-done.4 = s32[128]{0:T(128)S(1)} collective-permute-done((s32[128]{0:T(128)S(1)}, s32[128]{0:T(128)S(1)}, u32[]{:S(2)}, u32[]{:S(2)}) %collective-permute-start.4) | collective-permute-done | bytes 544 | tf_op jit(solution)/shard_map/ppermute | solution.py:22
  122.7 0.0 collective-permute-done.5
  122.7 0.9 fusion.15
  123.6 0.0 collective-permute-done.8
  123.6 0.3 fusion.18
  123.9 1.9 collective-permute-start.9
  125.9 7.4 %collective-permute-done.9 = f32[128,1152]{1,0:T(8,128)S(1)} collective-permute-done((f32[128,1152]{1,0:T(8,128)S(1)}, f32[128,1152]{1,0:T(8,128)S(1)}, u32[]{:S(2)}, u32[]{:S(2)}) %collective-permute-start.9) | collective-permute-done | bytes 589856 | tf_op jit(solution)/shard_map/ppermute | solution.py:22
  133.3 0.0 copy-start.3
  133.3 0.2 multiply_reduce_fusion
  133.5 0.6 copy-done.3
  134.1 0.5 copy-done.18
  134.6 2.5 fusion
  137.1 0.0 reduce-scatter.6.cloned.1.call-update
  137.1 0.0 copy-start.1
  137.1 1.3 dynamic-slice.2
  139.1 1.4 fusion.16
  140.5 1.3 convolution_add_fusion.2
  141.9 0.0 copy-start.4
  141.9 0.0 copy-start.16
  141.9 0.0 copy-start.19
  141.9 1.2 convolution_add_fusion.1
  143.1 1.2 add_add_fusion
  144.3 0.0 copy-done.1
  144.3 1.1 multiply_reduce_fusion.1
  145.5 1.0 subtract_divide_fusion
  146.5 0.0 copy-done.19
  146.5 1.8 fusion.21
  148.3 60.8 %reduce-scatter.6.cloned.1.call-done = bf16[1152,72]{0,1:T(8,128)(2,1)} async-done(((bf16[1152,1152]{0,1:T(8,128)(2,1)}), bf16[1152,72]{0,1:T(8,128)(2,1)}) %reduce-scatter.6.cloned.1.call-update) | async-done | bytes 165904
  209.1 238.6 %all-reduce.3 = f32[1152,72]{0,1:T(8,128)S(1)} all-reduce(bf16[1152,72]{0,1:T(8,128)(2,1)} %reduce-scatter.6.cloned.1.call-done), channel_id=3, replica_groups=mesh['blk'=48,'group'=16] {'blk'}, use_global_device_ids=true, to_apply=%region_5.6.clone | all-reduce | flops 82944 | bytes 497664
  447.7 0.1 constant_dynamic-slice_fusion
  447.7 0.7 copy.11
  (30 shorter events, 0.1 us)
Async XLA Ops:
  7.2 3.8 copy-start
  7.2 201.9 %reduce-scatter.6.cloned.1.call-start = ((), (), s32[]{:S(2)}) async-start(), calls=%async_computation.1 | async-start | bytes 2820096
  8.7 4.0 copy-start.14
  12.6 120.9 %copy-start.15 = (f32[128]{0:T(128)}, f32[128]{0:T(128)S(1)}, u32[]{:S(2)}) copy-start(f32[128]{0:T(128)S(1)} %add_sqrt_fusion) | copy-start | bytes 1540
  12.7 75.1 %copy-start.2 = (bf16[128,1152]{1,0:T(8,128)(2,1)}, bf16[128,1152]{1,0:T(8,128)(2,1)S(1)}, u32[]{:S(2)}) copy-start(bf16[128,1152]{1,0:T(8,128)(2,1)S(1)} %fusion.20) | copy-start | bytes 884740
  13.6 55.7 %copy-start.9 = (f32[128,128]{0,1:T(8,128)}, f32[128,128]{0,1:T(8,128)S(1)}, u32[]{:S(2)}) copy-start(f32[128,128]{0,1:T(8,128)S(1)} %get-tuple-element.21) | copy-start | bytes 196612
  13.9 55.4 %collective-permute-start.6 = (f32[128,1152]{1,0:T(8,128)S(1)}, f32[128,1152]{1,0:T(8,128)S(1)}, u32[]{:S(2)}, u32[]{:S(2)}) collective-permute-start(f32[128,1152]{1,0:T(8,128)S(1)} %convolution_multiply_fusion.3), channel_id=1, source_target_pairs={{0,16},{16,32},{32,48},{48,64},{64,80},{80,96},{96,112},{112,128},... | collective-permute-start | bytes 1769480 | tf_op jit(solution)/shard_map/ppermute | solution.py:22
  18.2 50.3 %collective-permute-start.1 = (bf16[128,1152]{1,0:T(8,128)(2,1)S(1)}, bf16[128,1152]{1,0:T(8,128)(2,1)S(1)}, u32[]{:S(2)}, u32[]{:S(2)}) collective-permute-start(bf16[128,1152]{1,0:T(8,128)(2,1)S(1)} %fusion.20), channel_id=1, source_target_pairs={{0,16},{16,32},{32,48},{48,64},{64,80},{80,96},{96,112},{112,128},... | collective-permute-start | bytes 884744 | tf_op jit(solution)/shard_map/ppermute | solution.py:22
  22.5 46.0 %collective-permute-start = (s32[128]{0:T(128)S(1)}, s32[128]{0:T(128)S(1)}, u32[]{:S(2)}, u32[]{:S(2)}) collective-permute-start(s32[128]{0:T(128)S(1)} %copy-done.14), channel_id=1, source_target_pairs={{0,16},{16,32},{32,48},{48,64},{64,80},{80,96},{96,112},{112,128},... | collective-permute-start | bytes 1544 | tf_op jit(solution)/shard_map/ppermute | solution.py:22
  68.4 55.2 %copy-start.6 = (bf16[128,1152]{1,0:T(8,128)(2,1)}, bf16[128,1152]{1,0:T(8,128)(2,1)S(1)}, u32[]{:S(2)}) copy-start(bf16[128,1152]{1,0:T(8,128)(2,1)S(1)} %collective-permute-done.1) | copy-start | bytes 884740
  69.3 0.6 copy-start.10
  70.2 17.4 %collective-permute-start.7 = (f32[128,1152]{1,0:T(8,128)S(1)}, f32[128,1152]{1,0:T(8,128)S(1)}, u32[]{:S(2)}, u32[]{:S(2)}) collective-permute-start(f32[128,1152]{1,0:T(8,128)S(1)} %fusion.1), channel_id=1, source_target_pairs={{0,1},{1,2},{2,3},{3,4},{4,5},{5,6},{6,7},{7,8},{8,9},{9,10},{10,1... | collective-permute-start | bytes 1769480 | tf_op jit(solution)/shard_map/ppermute | solution.py:22
  72.1 14.6 %collective-permute-start.3 = (bf16[128,1152]{1,0:T(8,128)(2,1)S(1)}, bf16[128,1152]{1,0:T(8,128)(2,1)S(1)}, u32[]{:S(2)}, u32[]{:S(2)}) collective-permute-start(bf16[128,1152]{1,0:T(8,128)(2,1)S(1)} %collective-permute-done.1), channel_id=1, source_target_pairs={{0,1},{1,2},{2,3},{3,4},{4,5},{5,6},{6,7},{7,8},{8,9},{9,10},{10,1... | collective-permute-start | bytes 884744 | tf_op jit(solution)/shard_map/ppermute | solution.py:22
  75.7 11.1 %collective-permute-start.2 = (s32[128]{0:T(128)S(1)}, s32[128]{0:T(128)S(1)}, u32[]{:S(2)}, u32[]{:S(2)}) collective-permute-start(s32[128]{0:T(128)S(1)} %collective-permute-done), channel_id=1, source_target_pairs={{0,1},{1,2},{2,3},{3,4},{4,5},{5,6},{6,7},{7,8},{8,9},{9,10},{10,1... | collective-permute-start | bytes 1544 | tf_op jit(solution)/shard_map/ppermute | solution.py:22
  86.8 46.5 %copy-start.7 = (bf16[128,1152]{1,0:T(8,128)(2,1)}, bf16[128,1152]{1,0:T(8,128)(2,1)S(1)}, u32[]{:S(2)}) copy-start(bf16[128,1152]{1,0:T(8,128)(2,1)S(1)} %collective-permute-done.3) | copy-start | bytes 884740
  87.6 45.7 %copy-start.11 = (f32[128,128]{0,1:T(8,128)}, f32[128,128]{0,1:T(8,128)S(1)}, u32[]{:S(2)}) copy-start(f32[128,128]{0,1:T(8,128)S(1)} %get-tuple-element.19) | copy-start | bytes 196612
  87.6 47.0 %copy-start.5 = (bf16[128,1152]{1,0:T(8,128)(2,1)S(1)}, bf16[128,1152]{1,0:T(8,128)(2,1)}, u32[]{:S(2)}) copy-start(bf16[128,1152]{1,0:T(8,128)(2,1)} %param.7) | copy-start | bytes 884740
  87.9 35.8 %collective-permute-start.8 = (f32[128,1152]{1,0:T(8,128)S(1)}, f32[128,1152]{1,0:T(8,128)S(1)}, u32[]{:S(2)}, u32[]{:S(2)}) collective-permute-start(f32[128,1152]{1,0:T(8,128)S(1)} %fusion.17), channel_id=1, source_target_pairs={{0,752},{16,0},{32,16},{48,32},{64,48},{80,64},{96,80},{112,96},{1... | collective-permute-start | bytes 1769480 | tf_op jit(solution)/shard_map/ppermute | solution.py:22
  89.8 32.9 %collective-permute-start.5 = (bf16[128,1152]{1,0:T(8,128)(2,1)S(1)}, bf16[128,1152]{1,0:T(8,128)(2,1)S(1)}, u32[]{:S(2)}, u32[]{:S(2)}) collective-permute-start(bf16[128,1152]{1,0:T(8,128)(2,1)S(1)} %collective-permute-done.3), channel_id=1, source_target_pairs={{0,752},{16,0},{32,16},{48,32},{64,48},{80,64},{96,80},{112,96},{1... | collective-permute-start | bytes 884744 | tf_op jit(solution)/shard_map/ppermute | solution.py:22
  91.7 31.0 %collective-permute-start.4 = (s32[128]{0:T(128)S(1)}, s32[128]{0:T(128)S(1)}, u32[]{:S(2)}, u32[]{:S(2)}) collective-permute-start(s32[128]{0:T(128)S(1)} %collective-permute-done.2), channel_id=1, source_target_pairs={{0,752},{16,0},{32,16},{48,32},{64,48},{80,64},{96,80},{112,96},{1... | collective-permute-start | bytes 1544 | tf_op jit(solution)/shard_map/ppermute | solution.py:22
  122.7 10.5 %copy-start.17 = (s32[128]{0:T(128)}, s32[128]{0:T(128)S(1)}, u32[]{:S(2)}) copy-start(s32[128]{0:T(128)S(1)} %collective-permute-done.4) | copy-start | bytes 1540
  122.7 0.9 copy-start.20
  123.6 9.6 %copy-start.12 = (f32[128,128]{0,1:T(8,128)}, f32[128,128]{0,1:T(8,128)S(1)}, u32[]{:S(2)}) copy-start(f32[128,128]{0,1:T(8,128)S(1)} %get-tuple-element.17) | copy-start | bytes 196612
  123.9 9.3 %collective-permute-start.9 = (f32[128,1152]{1,0:T(8,128)S(1)}, f32[128,1152]{1,0:T(8,128)S(1)}, u32[]{:S(2)}, u32[]{:S(2)}) collective-permute-start(f32[128,1152]{1,0:T(8,128)S(1)} %fusion.18), channel_id=1, source_target_pairs={{0,15},{1,0},{2,1},{3,2},{4,3},{5,4},{6,5},{7,6},{8,7},{9,8},{10,9... | collective-permute-start | bytes 1769480 | tf_op jit(solution)/shard_map/ppermute | solution.py:22
  133.3 0.8 copy-start.3
  134.1 0.5 copy-start.18
  137.1 7.2 %copy-start.1 = (bf16[128,1152]{1,0:T(8,128)(2,1)S(1)}, bf16[128,1152]{1,0:T(8,128)(2,1)}, u32[]{:S(2)}) copy-start(bf16[128,1152]{1,0:T(8,128)(2,1)} %param.6) | copy-start | bytes 884740
  139.1 2.8 copy-start.8
  139.1 5.2 %copy-start.13 = (f32[128,128]{0,1:T(8,128)S(1)}, f32[128,128]{0,1:T(8,128)}, u32[]{:S(2)}) copy-start(f32[128,128]{0,1:T(8,128)} %copy-done.12) | copy-start | bytes 196612
  139.1 5.2 %copy-start.21 = (bf16[128,1152]{1,0:T(8,128)(2,1)S(1)}, bf16[128,1152]{1,0:T(8,128)(2,1)}, u32[]{:S(2)}) copy-start(bf16[128,1152]{1,0:T(8,128)(2,1)} %copy-done.20) | copy-start | bytes 884740
  141.9 4.6 %copy-start.4 = (f32[128,1152]{1,0:T(8,128)S(1)}, f32[128,1152]{1,0:T(8,128)}, u32[]{:S(2)}) copy-start(f32[128,1152]{1,0:T(8,128)} %copy-done.3) | copy-start | bytes 1769476
  141.9 4.6 %copy-start.16 = (f32[128]{0:T(128)S(1)}, f32[128]{0:T(128)}, u32[]{:S(2)}) copy-start(f32[128]{0:T(128)} %copy-done.15) | copy-start | bytes 1540
  141.9 4.6 %copy-start.19 = (f32[128]{0:T(128)S(1)}, f32[128]{0:T(128)}, u32[]{:S(2)}) copy-start(f32[128]{0:T(128)} %copy-done.18) | copy-start | bytes 1540
Sparse Core Ops, SparseCore 0:
  137.2 71.8 reduce-scatter.5
where the time goes:
time: 456 us; the launch traced here: 455 us
  blocking collectives  239 us (52%)
  waiting for transfers between devices  148 us (32%)
  starting transfers between devices  27.9 us (6%)
  between operations  16.5 us (4%)
  matrix products  15.5 us (3%)
  other arithmetic  4.77 us (1%)
    unnamed x1, blocking collectives  239 us
    ppermute x10, waiting for transfers between devices, shifted(): lax.ppermute(value, axis, [(i, (i + by) % length) for i in range(length)])  87.3 us
    unnamed x2, waiting for transfers between devices  60.9 us
    ppermute x10, starting transfers between devices, shifted(): lax.ppermute(value, axis, [(i, (i + by) % length) for i in range(length)])  27.9 us
  transfers between devices with their start and end apart: 11, of which 5 were waited for; matrix products, arithmetic and copies ran while one was open for 3% of the time, Pallas kernels for 0%

commit v1 on v0

v1 whole, which is shorter than its diff:
```python
import jax
import jax.numpy as jnp
from jax import lax
from jax.experimental import pallas as pl
from jax.experimental.pallas import tpu as pltpu
from jax.sharding import Mesh
from jax.sharding import PartitionSpec as P

EPS = 1e-06
BF16 = jnp.bfloat16
F32 = jnp.float32
BLK = ("yh", "z")
GROUP = ("yl", "x", "core")
QUAD = ("yl", "core")
ALL = BLK + GROUP
N_YL, N_X, N_CORE = 2, 4, 2
TEXT_FLOPS = 12 * 10**9
VMEM_BYTES = 12 * 1024 * 1024


def shifted(value, axes, by):
    length = lax.axis_size(axes)
    return lax.ppermute(value, axes, [(i, (i + by) % length) for i in range(length)])


def kernel_call(kernel, out_shape, flops, scalars, arrays, scratch=()):
    moved = sum(v.size * v.dtype.itemsize for v in arrays)
    moved += sum(v.size * v.dtype.itemsize for v in jax.tree.leaves(out_shape))
    return pl.pallas_call(
        kernel,
        out_shape=out_shape,
        in_specs=[pl.BlockSpec(memory_space=pltpu.SMEM)] * len(scalars)
        + [pl.BlockSpec(memory_space=pltpu.VMEM)] * len(arrays),
        out_specs=jax.tree.map(lambda _: pl.BlockSpec(memory_space=pltpu.VMEM), out_shape),
        scratch_shapes=scratch,
        compiler_params=pltpu.CompilerParams(vmem_limit_bytes=VMEM_BYTES),
        cost_estimate=pl.CostEstimate(flops=flops, bytes_accessed=moved, transcendentals=0),
    )(*scalars, *arrays)


def dot_nt(left, right):
    return lax.dot_general(left, right, (((1,), (1,)), ((), ())), preferred_element_type=F32)


def lengths_of(vectors):
    return jnp.sqrt(jnp.sum(vectors * vectors, axis=-1, keepdims=True) + EPS)


def after(value, *earlier):
    return lax.optimization_barrier((value,) + earlier)[0]


def homes():
    n_group = N_YL * N_X * N_CORE
    n_blk = lax.axis_size("yh") * lax.axis_size("z")
    b = lax.axis_index("yh") * lax.axis_size("z") + lax.axis_index("z")
    g = (lax.axis_index("yl") * N_X + lax.axis_index("x")) * N_CORE + lax.axis_index("core")
    return b, g, n_blk, n_group


def offsets_of(ids):
    b, g, n_blk, n_group = homes()
    rows = ids.shape[1]
    total = n_blk * n_group * rows
    own = (b * n_group + g) * rows + lax.broadcasted_iota(jnp.int32, ids.shape, 1)
    step = ids - own
    step = jnp.where(step < 0, step + total, step)
    code = jnp.where(step == 0, 0.0, float(n_group + 1))
    code = jnp.where(step == rows, 1.0, code)
    return jnp.where(step == n_group * rows, float(n_group), code)


def with_offsets(units, ids):
    code = jnp.broadcast_to(offsets_of(ids), (8, ids.shape[1]))
    rest = jnp.zeros((8, units.shape[1] - ids.shape[1]), F32)
    return jnp.concatenate([units, jnp.concatenate([code, rest], axis=1)], axis=0).astype(BF16)


def split_block(block):
    rows = block.shape[0] - 8
    code = block[...].astype(F32)[rows : rows + 1, 0:rows]
    return block[0:rows, :], code


def met_pairs(image_code, text_code, apart, total):
    rows = image_code.shape[1]
    row = lax.broadcasted_iota(jnp.int32, (rows, rows), 0)
    column = lax.broadcasted_iota(jnp.int32, (rows, rows), 1)
    step = image_code - text_code + apart.astype(F32)
    same = (step == 0.0) | (step == float(total)) | (step == -float(total))
    return (row == column) & same


def signed_logit(score, match, scale, bias):
    logit = scale * score + bias
    return jnp.where(match, -logit, logit)


def slope_of(value, match):
    slope = 1.0 / (1.0 + jnp.exp(-value))
    return jnp.where(match, -slope, slope).astype(BF16)


def softplus(value):
    return jnp.maximum(value, 0.0) + jnp.log1p(jnp.exp(-jnp.abs(value)))


def block_kernel(img, feats, ids, img_block, txt_block):
    wide = img[...].astype(F32)
    img_block[...] = with_offsets(wide / lengths_of(wide), ids[...])
    txt_block[...] = with_offsets(feats[...].astype(F32), ids[...])


def text_kernel(feats, head, unit, length):
    pre = jnp.dot(feats[...], head[...], preferred_element_type=F32)
    size = lengths_of(pre)
    unit[...] = pre / size
    length[...] = size


def text_side_kernel(scale_log, logit_bias, unit, length, img, img_g, img_b, img_bg, turned):
    scale = jnp.exp(jnp.full((1, 1), scale_log[0], F32))
    bias = logit_bias[0]
    b, g, n_blk, n_group = homes()
    next_b = lax.rem(b + 1, n_blk) - b
    next_g = lax.rem(g + 1, n_group) - g
    aparts = (0 * b, next_g, next_b * n_group, next_b * n_group + next_g)
    own = unit[...]
    text = own.astype(BF16)
    total = jnp.zeros(own.shape, F32)
    own_code = split_block(img)[1]
    for block, apart in zip((img, img_g, img_b, img_bg), aparts):
        images, code = split_block(block)
        match = met_pairs(code, own_code, apart, n_blk * n_group)
        value = signed_logit(dot_nt(text, images), match, scale, bias)
        total += jnp.dot(slope_of(value, match), images, preferred_element_type=F32)
    grad = scale * total
    result = (grad - own * jnp.sum(own * grad, axis=-1, keepdims=True)) / length[...]
    columns = result.T
    part = columns.shape[0] // (N_YL * N_X * N_CORE)
    for yl in range(N_YL):
        for x in range(N_X):
            for core in range(N_CORE):
                at = ((yl * N_X + x) * N_CORE + core) * part
                turned[(yl * N_CORE + core) * N_X + x] = columns[at : at + part].astype(BF16)


def image_side_kernel(
    scale_log,
    logit_bias,
    img,
    unit,
    txt,
    txt_g,
    txt_b,
    txt_bg,
    turned,
    head,
    grad_out,
    loss_out,
    text_out,
):
    scale = jnp.exp(jnp.full((1, 1), scale_log[0], F32))
    bias = logit_bias[0]
    b, g, n_blk, n_group = homes()
    last_b = b - lax.rem(b + n_blk - 1, n_blk)
    last_g = g - lax.rem(g + n_group - 1, n_group)
    aparts = (0 * b, last_g, last_b * n_group, last_b * n_group + last_g)
    wide = img[...].astype(F32)
    size = lengths_of(wide)
    own = wide / size
    image = own.astype(BF16)
    total = jnp.zeros(wide.shape, F32)
    loss = jnp.zeros((wide.shape[0], 1), F32)
    own_code = split_block(txt)[1]
    for block, apart in zip((txt, txt_g, txt_b, txt_bg), aparts):
        feats, code = split_block(block)
        if block is txt:
            texts = unit[...].astype(BF16)
        else:
            pre = jnp.dot(feats, head[...], preferred_element_type=F32)
            texts = (pre / lengths_of(pre)).astype(BF16)
        match = met_pairs(own_code, code, apart, n_blk * n_group)
        value = signed_logit(dot_nt(image, texts), match, scale, bias)
        loss += jnp.sum(softplus(value), axis=-1, keepdims=True)
        total += jnp.dot(slope_of(value, match), texts, preferred_element_type=F32)
    grad = scale * total
    grad_out[...] = (grad - own * jnp.sum(own * grad, axis=-1, keepdims=True)) / size
    loss_out[...] = jnp.broadcast_to(loss, (loss.shape[0], loss.shape[0])).T[0:1]
    blocks = [
        turned[(yl * N_CORE + core) * N_X + x].astype(F32)
        for yl in range(N_YL)
        for x in range(N_X)
        for core in range(N_CORE)
    ]
    delta = jnp.concatenate(blocks, axis=0).T.astype(BF16)
    text_out[...] = dot_nt(delta, head[...])


def head_kernel(place, met, feats, feats_c, feats_y, feats_cy, out):
    m = place[0]
    across = m + 1 - 2 * lax.rem(m, 2)
    total = jnp.zeros((met.shape[1] * met.shape[2], feats.shape[1]), F32)
    for at, block in (
        (m, feats),
        (across, feats_c),
        (lax.rem(m + 2, 4), feats_y),
        (lax.rem(across + 2, 4), feats_cy),
    ):
        columns = met[at].astype(F32).reshape(total.shape[0], met.shape[3]).astype(BF16)
        total += jnp.dot(columns, block[...], preferred_element_type=F32)
    out[...] = total.reshape(out.shape).astype(BF16)


def pack_kernel(parts, out, wide, tail, packed):
    columns = jnp.sum(parts[...].astype(F32), axis=0)
    n, depth, lanes = wide.shape
    width = columns.shape[0]
    over = lanes - width
    left = width - over
    half = depth // 2
    wide[...] = jnp.concatenate([columns, columns[:over]], axis=0).T.reshape(wide.shape)
    copies = [columns[over:]] * (lanes // left)
    tail[...] = jnp.concatenate(copies, axis=0).T.reshape(tail.shape)
    lane = lax.broadcasted_iota(jnp.int32, (n, half, lanes), 2)
    packed[:, 0:half, :] = jnp.where(lane < width, wide[:, 0:half, :], wide[:, half:depth, :])
    short = half // 3
    lane = lax.broadcasted_iota(jnp.int32, (n, short, lanes), 2)
    rest = tail[:, half : half + short, :]
    for k in (1, 2):
        piece = tail[:, half + k * short : half + (k + 1) * short, :]
        rest = jnp.where(lane >= k * left, piece, rest)
    packed[:, half : half + short, :] = rest
    out[...] = packed[...].astype(BF16)


def unpack_kernel(parts, out):
    total = jnp.sum(parts[...].astype(F32), axis=0)
    depth, width = out.shape
    lanes = total.shape[1]
    over = lanes - width
    left = width - over
    half = depth // 2
    short = half // 3
    out[0:half, :] = total[0:half, 0:width]
    out[half:depth, 0:over] = total[0:half, width:lanes]
    for k in range(3):
        at = half + k * short
        out[at : at + short, over:width] = total[half : half + short, k * left : (k + 1) * left]


def body(image_emb, text_feats, text_head, scale_log, logit_bias, pair_index):
    rows, width = image_emb.shape
    n_blk = lax.axis_size(BLK)
    ids = pair_index.reshape(1, rows)
    like = jax.ShapeDtypeStruct
    score = 2 * rows * rows * width

    block = like((rows + 8, width), BF16)
    img, txt = kernel_call(block_kernel, (block, block), 0, (), (image_emb, text_feats, ids))
    img_b = shifted(img, BLK, -1)
    txt_b = shifted(txt, BLK, 1)
    img_g = shifted(img, GROUP, -1)
    txt_g = shifted(after(txt, img_g), GROUP, 1)
    unit, length = kernel_call(
        text_kernel,
        (like((rows, width), F32), like((rows, 1), F32)),
        TEXT_FLOPS,
        (),
        (after(text_feats, img_g), text_head),
    )
    img_b, txt_b = lax.optimization_barrier((img_b, txt_b, unit, txt_g))[:2]
    img_bg = shifted(img_b, GROUP, -1)
    swap = [(0, 1), (1, 0)]
    feats_y = lax.ppermute(after(text_feats, img_b), "yl", swap)

    part = width // (N_YL * N_X * N_CORE)
    turned = kernel_call(
        text_side_kernel,
        like((N_YL * N_CORE * N_X, part, rows), BF16),
        8 * score,
        (scale_log, logit_bias),
        (unit, length, img, img_g, img_b, img_bg),
    )

    late_txt, late_b = lax.optimization_barrier((text_feats, txt_b, turned))[:2]
    feats_c = lax.ppermute(late_txt, "core", swap)
    feats_cy = lax.ppermute(feats_y, "core", swap)
    txt_bg = shifted(late_b, GROUP, 1)
    place = lax.axis_index(QUAD).reshape(1)
    quads = turned.reshape(N_YL * N_CORE, N_X, part, rows)
    met = lax.all_to_all(quads, QUAD, 0, 0)
    partial = kernel_call(
        head_kernel,
        like((N_X, part, width), BF16),
        2 * 4 * rows * width * N_X * part,
        (place,),
        (met, text_feats, feats_c, feats_y, feats_cy),
    )
    partial = lax.all_to_all(after(partial, txt_bg), "x", 0, 0)
    depth = width // n_blk
    packed = kernel_call(
        pack_kernel,
        like((n_blk, 16, 128), BF16),
        0,
        (),
        (partial,),
        (
            pltpu.VMEM((n_blk, depth, 128), F32),
            pltpu.VMEM((n_blk, depth, 128), F32),
            pltpu.VMEM((n_blk, 16, 128), F32),
        ),
    )
    summed = lax.all_to_all(packed, BLK, 0, 0)
    head_grad = kernel_call(unpack_kernel, like((depth, part), F32), 0, (), (summed,))

    image_grad, row_loss, text_grad = kernel_call(
        image_side_kernel,
        (like((rows, width), F32), like((1, rows), F32), like((rows, width), F32)),
        8 * score + 8 * rows * width * width,
        (scale_log, logit_bias),
        (
            after(image_emb, packed),
            unit,
            txt,
            txt_g,
            txt_b,
            txt_bg,
            turned,
            text_head,
        ),
    )
    return (image_grad, text_grad, head_grad, row_loss.reshape(rows))


def solution(mesh):
    fine = Mesh(mesh.devices.reshape(4, 12, N_YL, N_X, N_CORE), ALL)
    rows = P(ALL, None)
    return jax.shard_map(
        body,
        mesh=fine,
        in_specs=(rows, rows, P(), P(), P(), P(ALL)),
        out_specs=(rows, rows, P(BLK, GROUP), P(ALL)),
        check_vma=False,
    )
```

time: 456 us -> 115 us (0.25)
  the two profiles are of different devices: /device:TPU:8 before, /device:TPU:2 now
where the time goes in v1:
time: 115 us
  starting transfers between devices  46.3 us (40%)
  waiting for transfers between devices  31.2 us (27%)
  Pallas kernels  15 us (13%)
  blocking collectives  14.9 us (13%)
  local copies, waits for them, and re-layouts  5.1 us (4%)
  between operations  2.11 us (2%)
    ppermute x6, starting transfers between devices, shifted(): lax.ppermute(value, axes, [(i, (i + by) % length) for i in range(length)])  28.6 us
    ppermute x6, waiting for transfers between devices, shifted(): lax.ppermute(value, axes, [(i, (i + by) % length) for i in range(length)])  21.5 us
    pallas_call x7, Pallas kernels, kernel_call(): pl.pallas_call(kernel, out_shape=out_shape, in_specs=[pl.BlockSpec(memory...  15 us
    all_to_all x1, blocking collectives, body(): partial = lax.all_to_all(after(partial, txt_bg), 'x', 0, 0)  14.9 us
    all_to_all x1, waiting for transfers between devices, body(): summed = lax.all_to_all(packed, BLK, 0, 0)  8.53 us
    all_to_all x1, starting transfers between devices, body(): summed = lax.all_to_all(packed, BLK, 0, 0)  7.56 us
    unnamed x10, local copies, waits for them, and re-layouts  5.1 us
    all_to_all x1, starting transfers between devices, body(): met = lax.all_to_all(quads, QUAD, 0, 0)  3.58 us
  transfers between devices with their start and end apart: 11, of which 6 were waited for; matrix products, arithmetic and copies ran while one was open for 0% of the time, Pallas kernels for 10%

profile of v1, /device:TPU:2, one launch (start us, length us, event | category | flops | bytes accessed | tf_op | source)
XLA Modules:
  0.0 114.6 jit_solution(3787019644702316216)
XLA Ops:
  0.6 0.0 copy-start
  0.6 1.0 copy-done
  1.6 0.0 copy-start.2
  1.6 0.7 copy-done.2
  2.3 1.1 shard_map.93
  3.4 1.9 %collective-permute-start = (bf16[136,1152]{1,0:T(8,128)(2,1)S(1)}, bf16[136,1152]{1,0:T(8,128)(2,1)S(1)}, u32[]{:S(2)}, u32[]{:S(2)}) collective-permute-start(bf16[136,1152]{1,0:T(8,128)(2,1)S(1)} %get-tuple-element.20.img), channel_id=1, source_target_pairs={{0,15},{1,0},{2,1},{3,2},{4,3},{5,4},{6,5},{7,6},{8,7},{9,8},{10,9... | collective-permute-start | bytes 940040 | tf_op jit(solution)/shard_map/ppermute | solution.py:23
  5.3 18.3 %collective-permute-start.1 = (bf16[136,1152]{1,0:T(8,128)(2,1)S(1)}, bf16[136,1152]{1,0:T(8,128)(2,1)S(1)}, u32[]{:S(2)}, u32[]{:S(2)}) collective-permute-start(bf16[136,1152]{1,0:T(8,128)(2,1)S(1)} %get-tuple-element.20.img), channel_id=1, source_target_pairs={{0,752},{16,0},{32,16},{48,32},{64,48},{80,64},{96,80},{112,96},{1... | collective-permute-start | bytes 940040 | tf_op jit(solution)/shard_map/ppermute | solution.py:23
  23.6 1.9 %collective-permute-start.2 = (bf16[136,1152]{1,0:T(8,128)(2,1)S(1)}, bf16[136,1152]{1,0:T(8,128)(2,1)S(1)}, u32[]{:S(2)}, u32[]{:S(2)}) collective-permute-start(bf16[136,1152]{1,0:T(8,128)(2,1)S(1)} %get-tuple-element.25.txt), channel_id=1, source_target_pairs={{0,16},{16,32},{32,48},{48,64},{64,80},{80,96},{96,112},{112,128},... | collective-permute-start | bytes 940040 | tf_op jit(solution)/shard_map/ppermute | solution.py:23
  25.5 0.0 collective-permute-done.img_g
  25.5 2.1 %collective-permute-start.3 = (bf16[136,1152]{1,0:T(8,128)(2,1)S(1)}, bf16[136,1152]{1,0:T(8,128)(2,1)S(1)}, u32[]{:S(2)}, u32[]{:S(2)}) collective-permute-start(bf16[136,1152]{1,0:T(8,128)(2,1)S(1)} %get-tuple-element.25.txt), channel_id=1, source_target_pairs={{0,1},{1,2},{2,3},{3,4},{4,5},{5,6},{6,7},{7,8},{8,9},{9,10},{10,1... | collective-permute-start | bytes 940040 | tf_op jit(solution)/shard_map/ppermute | solution.py:23
  27.7 0.0 copy-start.3
  27.7 1.7 %copy-done.3 = bf16[1152,1152]{1,0:T(8,128)(2,1)S(1)} copy-done((bf16[1152,1152]{1,0:T(8,128)(2,1)S(1)}, bf16[1152,1152]{1,0:T(8,128)(2,1)}, u32[]{:S(2)}) %copy-start.3) | copy-done | bytes 2654232
  29.4 1.7 %shard_map.94 = (f32[128,1152]{1,0:T(8,128)S(1)}, f32[128,1]{1,0:T(8,128)S(1)}) custom-call(bf16[128,1152]{1,0:T(8,128)(2,1)} %feats.4, bf16[1152,1152]{1,0:T(8,128)(2,1)S(1)} %copy-done.3), custom_call_target="tpu_custom_call" | custom-call | flops 12000000000 | bytes 3539456 | tf_op jit(solution)/shard_map/pallas_call | solution.py:29
  31.1 3.4 %collective-permute-done.1.img_b = bf16[136,1152]{1,0:T(8,128)(2,1)S(1)} collective-permute-done((bf16[136,1152]{1,0:T(8,128)(2,1)S(1)}, bf16[136,1152]{1,0:T(8,128)(2,1)S(1)}, u32[]{:S(2)}, u32[]{:S(2)}) %collective-permute-start.1) | collective-permute-done | bytes 313376 | tf_op jit(solution)/shard_map/ppermute | solution.py:23
  34.6 11.0 %collective-permute-done.2.txt_b = bf16[136,1152]{1,0:T(8,128)(2,1)S(1)} collective-permute-done((bf16[136,1152]{1,0:T(8,128)(2,1)S(1)}, bf16[136,1152]{1,0:T(8,128)(2,1)S(1)}, u32[]{:S(2)}, u32[]{:S(2)}) %collective-permute-start.2) | collective-permute-done | bytes 313376 | tf_op jit(solution)/shard_map/ppermute | solution.py:23
  45.5 0.0 collective-permute-done.3.txt_g
  45.5 1.9 %collective-permute-start.4 = (bf16[136,1152]{1,0:T(8,128)(2,1)S(1)}, bf16[136,1152]{1,0:T(8,128)(2,1)S(1)}, u32[]{:S(2)}, u32[]{:S(2)}) collective-permute-start(bf16[136,1152]{1,0:T(8,128)(2,1)S(1)} %collective-permute-done.1.img_b), channel_id=1, source_target_pairs={{0,15},{1,0},{2,1},{3,2},{4,3},{5,4},{6,5},{7,6},{8,7},{9,8},{10,9... | collective-permute-start | bytes 940040 | tf_op jit(solution)/shard_map/ppermute | solution.py:23
  47.5 1.9 %collective-permute-start.6 = (bf16[128,1152]{1,0:T(8,128)(2,1)}, bf16[128,1152]{1,0:T(8,128)(2,1)S(1)}, u32[]{:S(2)}, u32[]{:S(2)}) collective-permute-start(bf16[128,1152]{1,0:T(8,128)(2,1)} %feats.4), channel_id=1, source_target_pairs={{0,8},{8,0},{1,9},{9,1},{2,10},{10,2},{3,11},{11,3},{4,12},{12,4},... | collective-permute-start | bytes 884744 | tf_op jit(solution)/shard_map/ppermute | solution.py:275
  50.7 1.2 %collective-permute-done.4.img_bg = bf16[136,1152]{1,0:T(8,128)(2,1)S(1)} collective-permute-done((bf16[136,1152]{1,0:T(8,128)(2,1)S(1)}, bf16[136,1152]{1,0:T(8,128)(2,1)S(1)}, u32[]{:S(2)}, u32[]{:S(2)}) %collective-permute-start.4) | collective-permute-done | bytes 313376 | tf_op jit(solution)/shard_map/ppermute | solution.py:23
  51.9 2.3 %shard_map.95.turned = bf16[16,72,128]{2,1,0:T(8,128)(2,1)} custom-call(f32[1]{0:T(128)S(6)} %copy.10.scale_log, f32[1]{0:T(128)S(6)} %copy.11.logit_bias, f32[128,1152]{1,0:T(8,128)S(1)} %get-tuple-element.22.unit, f32[128,1]{1,0:T(8,128)S(1)} %get-tuple-element.23.length, bf16[136,1152]{1,0:T(8,128)(2,1)S(1)} %get-tuple-element.20.img, ...), custom_call_target="tpu_custom_call" | custom-call | flops 301989888 | bytes 2138624 | tf_op jit(solution)/shard_map/pallas_call | solution.py:29
  54.2 0.0 copy-start.1
  54.2 3.6 %all-to-all-start = ((bf16[4,4,72,128]{3,2,1,0:T(8,128)(2,1)}), bf16[4,4,72,128]{3,2,1,0:T(8,128)(2,1)S(1)}, u32[]{:S(2)}, u32[]{:S(2)}) async-start(bf16[4,4,72,128]{3,2,1,0:T(8,128)(2,1)} %bitcast.2), calls=%async_computation | async-start | bytes 589824 | tf_op jit(solution)/shard_map/all_to_all | solution.py:292
  57.8 1.2 %collective-permute-done.6.feats_y = bf16[128,1152]{1,0:T(8,128)(2,1)S(1)} collective-permute-done((bf16[128,1152]{1,0:T(8,128)(2,1)}, bf16[128,1152]{1,0:T(8,128)(2,1)S(1)}, u32[]{:S(2)}, u32[]{:S(2)}) %collective-permute-start.6) | collective-permute-done | bytes 294944 | tf_op jit(solution)/shard_map/ppermute | solution.py:275
  59.0 2.7 %collective-permute-start.7 = (bf16[128,1152]{1,0:T(8,128)(2,1)S(1)}, bf16[128,1152]{1,0:T(8,128)(2,1)S(1)}, u32[]{:S(2)}, u32[]{:S(2)}) collective-permute-start(bf16[128,1152]{1,0:T(8,128)(2,1)S(1)} %collective-permute-done.6.feats_y), channel_id=1, source_target_pairs={{0,1},{1,0},{2,3},{3,2},{4,5},{5,4},{6,7},{7,6},{8,9},{9,8},{10,11... | collective-permute-start | bytes 884744 | tf_op jit(solution)/shard_map/ppermute | solution.py:288
  61.7 1.9 %collective-permute-start.5 = (bf16[128,1152]{1,0:T(8,128)(2,1)}, bf16[128,1152]{1,0:T(8,128)(2,1)S(1)}, u32[]{:S(2)}, u32[]{:S(2)}) collective-permute-start(bf16[128,1152]{1,0:T(8,128)(2,1)} %feats.4), channel_id=1, source_target_pairs={{0,1},{1,0},{2,3},{3,2},{4,5},{5,4},{6,7},{7,6},{8,9},{9,8},{10,11... | collective-permute-start | bytes 884744 | tf_op jit(solution)/shard_map/ppermute | solution.py:287
  63.7 2.4 %collective-permute-start.8 = (bf16[136,1152]{1,0:T(8,128)(2,1)S(1)}, bf16[136,1152]{1,0:T(8,128)(2,1)S(1)}, u32[]{:S(2)}, u32[]{:S(2)}) collective-permute-start(bf16[136,1152]{1,0:T(8,128)(2,1)S(1)} %collective-permute-done.2.txt_b), channel_id=1, source_target_pairs={{0,1},{1,2},{2,3},{3,4},{4,5},{5,6},{6,7},{7,8},{8,9},{9,10},{10,1... | collective-permute-start | bytes 940040 | tf_op jit(solution)/shard_map/ppermute | solution.py:23
  66.1 0.0 collective-permute-done.7.feats_cy
  66.1 0.0 collective-permute-done.5.feats_c
  66.1 0.0 all-to-all-done.met
  66.1 1.8 %shard_map.96 = bf16[4,72,1152]{2,1,0:T(8,128)(2,1)S(1)} custom-call(s32[1]{0:T(128)} %bitcast.place, bf16[4,4,72,128]{3,2,1,0:T(8,128)(2,1)S(1)} %all-to-all-done.met, bf16[128,1152]{1,0:T(8,128)(2,1)} %feats.4, bf16[128,1152]{1,0:T(8,128)(2,1)S(1)} %collective-permute-done.5.feats_c, bf16[128,1152]{1,0:T(8,128)(2,1)S(1)} %collective-permute-done.6.feats_y, ...), custom_call_target="tpu_custom_call" | custom-call | flops 339738624 | bytes 2138112 | tf_op jit(solution)/shard_map/pallas_call | solution.py:29
  67.9 5.9 %collective-permute-done.8.txt_bg = bf16[136,1152]{1,0:T(8,128)(2,1)S(1)} collective-permute-done((bf16[136,1152]{1,0:T(8,128)(2,1)S(1)}, bf16[136,1152]{1,0:T(8,128)(2,1)S(1)}, u32[]{:S(2)}, u32[]{:S(2)}) %collective-permute-start.8) | collective-permute-done | bytes 313376 | tf_op jit(solution)/shard_map/ppermute | solution.py:23
  73.8 14.9 %all_to_all.15.parts = bf16[4,72,1152]{2,1,0:T(8,128)(2,1)S(1)} all-to-all(bf16[4,72,1152]{2,1,0:T(8,128)(2,1)S(1)} %shard_map.96), channel_id=1, replica_groups=mesh['yh'=4,'z'=12,'yl'=2,'x'=4,'core'=2] {'x'}, dimensions={0} | all-to-all | bytes 1327104 | tf_op jit(solution)/shard_map/all_to_all | solution.py:300
  88.7 1.2 %shard_map.97 = bf16[48,16,128]{2,1,0:T(8,128)(2,1)} custom-call(bf16[4,72,1152]{2,1,0:T(8,128)(2,1)S(1)} %all_to_all.15.parts), custom_call_target="tpu_custom_call" | custom-call | bytes 860160 | tf_op jit(solution)/shard_map/pallas_call | solution.py:29
  89.8 7.6 %all-to-all-start.2 = ((bf16[48,16,128]{2,1,0:T(8,128)(2,1)}), bf16[48,16,128]{2,1,0:T(8,128)(2,1)S(1)}, u32[]{:S(2)}, u32[]{:S(2)}) async-start(bf16[48,16,128]{2,1,0:T(8,128)(2,1)} %shard_map.97), calls=%async_computation.2 | async-start | bytes 393216 | tf_op jit(solution)/shard_map/all_to_all | solution.py:314
  97.4 0.0 copy-done.1
  97.4 0.0 copy-start.4
  97.4 1.7 %copy-done.4 = bf16[1152,1152]{1,0:T(8,128)(2,1)S(1)} copy-done((bf16[1152,1152]{1,0:T(8,128)(2,1)S(1)}, bf16[1152,1152]{1,0:T(8,128)(2,1)}, u32[]{:S(2)}) %copy-start.4) | copy-done | bytes 2654232
  99.2 6.2 %shard_map.98 = (f32[128,1152]{1,0:T(8,128)}, f32[1,128]{1,0:T(1,128)}, f32[128,1152]{1,0:T(8,128)}) custom-call(f32[1]{0:T(128)S(6)} %copy.10.scale_log, f32[1]{0:T(128)S(6)} %copy.11.logit_bias, bf16[128,1152]{1,0:T(8,128)(2,1)S(1)} %copy-done.1, f32[128,1152]{1,0:T(8,128)S(1)} %get-tuple-element.22.unit, bf16[136,1152]{1,0:T(8,128)(2,1)S(1)} %get-tuple-element.25.txt, ...), custom_call_target="tpu_custom_call" | custom-call | flops 1660944384 | bytes 6267392 | tf_op jit(solution)/shard_map/pallas_call | solution.py:29
  105.3 8.5 %all-to-all-done.2.parts = bf16[48,16,128]{2,1,0:T(8,128)(2,1)S(1)} async-done(((bf16[48,16,128]{2,1,0:T(8,128)(2,1)}), bf16[48,16,128]{2,1,0:T(8,128)(2,1)S(1)}, u32[]{:S(2)}, u32[]{:S(2)}) %all-to-all-start.2) | async-done | bytes 196640 | tf_op jit(solution)/shard_map/all_to_all | solution.py:314
  113.9 0.7 shard_map.99
Async XLA Ops:
  0.6 1.0 copy-start
  1.6 0.7 copy-start.2
  3.4 22.1 %collective-permute-start = (bf16[136,1152]{1,0:T(8,128)(2,1)S(1)}, bf16[136,1152]{1,0:T(8,128)(2,1)S(1)}, u32[]{:S(2)}, u32[]{:S(2)}) collective-permute-start(bf16[136,1152]{1,0:T(8,128)(2,1)S(1)} %get-tuple-element.20.img), channel_id=1, source_target_pairs={{0,15},{1,0},{2,1},{3,2},{4,3},{5,4},{6,5},{7,6},{8,7},{9,8},{10,9... | collective-permute-start | bytes 940040 | tf_op jit(solution)/shard_map/ppermute | solution.py:23
  5.3 29.2 %collective-permute-start.1 = (bf16[136,1152]{1,0:T(8,128)(2,1)S(1)}, bf16[136,1152]{1,0:T(8,128)(2,1)S(1)}, u32[]{:S(2)}, u32[]{:S(2)}) collective-permute-start(bf16[136,1152]{1,0:T(8,128)(2,1)S(1)} %get-tuple-element.20.img), channel_id=1, source_target_pairs={{0,752},{16,0},{32,16},{48,32},{64,48},{80,64},{96,80},{112,96},{1... | collective-permute-start | bytes 940040 | tf_op jit(solution)/shard_map/ppermute | solution.py:23
  23.6 21.9 %collective-permute-start.2 = (bf16[136,1152]{1,0:T(8,128)(2,1)S(1)}, bf16[136,1152]{1,0:T(8,128)(2,1)S(1)}, u32[]{:S(2)}, u32[]{:S(2)}) collective-permute-start(bf16[136,1152]{1,0:T(8,128)(2,1)S(1)} %get-tuple-element.25.txt), channel_id=1, source_target_pairs={{0,16},{16,32},{32,48},{48,64},{64,80},{80,96},{96,112},{112,128},... | collective-permute-start | bytes 940040 | tf_op jit(solution)/shard_map/ppermute | solution.py:23
  25.5 20.0 %collective-permute-start.3 = (bf16[136,1152]{1,0:T(8,128)(2,1)S(1)}, bf16[136,1152]{1,0:T(8,128)(2,1)S(1)}, u32[]{:S(2)}, u32[]{:S(2)}) collective-permute-start(bf16[136,1152]{1,0:T(8,128)(2,1)S(1)} %get-tuple-element.25.txt), channel_id=1, source_target_pairs={{0,1},{1,2},{2,3},{3,4},{4,5},{5,6},{6,7},{7,8},{8,9},{9,10},{10,1... | collective-permute-start | bytes 940040 | tf_op jit(solution)/shard_map/ppermute | solution.py:23
  27.7 1.8 %copy-start.3 = (bf16[1152,1152]{1,0:T(8,128)(2,1)S(1)}, bf16[1152,1152]{1,0:T(8,128)(2,1)}, u32[]{:S(2)}) copy-start(bf16[1152,1152]{1,0:T(8,128)(2,1)} %head.3) | copy-start | bytes 7962628
  45.5 6.3 %collective-permute-start.4 = (bf16[136,1152]{1,0:T(8,128)(2,1)S(1)}, bf16[136,1152]{1,0:T(8,128)(2,1)S(1)}, u32[]{:S(2)}, u32[]{:S(2)}) collective-permute-start(bf16[136,1152]{1,0:T(8,128)(2,1)S(1)} %collective-permute-done.1.img_b), channel_id=1, source_target_pairs={{0,15},{1,0},{2,1},{3,2},{4,3},{5,4},{6,5},{7,6},{8,7},{9,8},{10,9... | collective-permute-start | bytes 940040 | tf_op jit(solution)/shard_map/ppermute | solution.py:23
  47.5 11.5 %collective-permute-start.6 = (bf16[128,1152]{1,0:T(8,128)(2,1)}, bf16[128,1152]{1,0:T(8,128)(2,1)S(1)}, u32[]{:S(2)}, u32[]{:S(2)}) collective-permute-start(bf16[128,1152]{1,0:T(8,128)(2,1)} %feats.4), channel_id=1, source_target_pairs={{0,8},{8,0},{1,9},{9,1},{2,10},{10,2},{3,11},{11,3},{4,12},{12,4},... | collective-permute-start | bytes 884744 | tf_op jit(solution)/shard_map/ppermute | solution.py:275
  54.2 43.2 %copy-start.1 = (bf16[128,1152]{1,0:T(8,128)(2,1)S(1)}, bf16[128,1152]{1,0:T(8,128)(2,1)}, u32[]{:S(2)}) copy-start(bf16[128,1152]{1,0:T(8,128)(2,1)} %img.2) | copy-start | bytes 884740
  54.2 11.9 %all-to-all-start = ((bf16[4,4,72,128]{3,2,1,0:T(8,128)(2,1)}), bf16[4,4,72,128]{3,2,1,0:T(8,128)(2,1)S(1)}, u32[]{:S(2)}, u32[]{:S(2)}) async-start(bf16[4,4,72,128]{3,2,1,0:T(8,128)(2,1)} %bitcast.2), calls=%async_computation | async-start | bytes 589824 | tf_op jit(solution)/shard_map/all_to_all | solution.py:292
  59.0 7.1 %collective-permute-start.7 = (bf16[128,1152]{1,0:T(8,128)(2,1)S(1)}, bf16[128,1152]{1,0:T(8,128)(2,1)S(1)}, u32[]{:S(2)}, u32[]{:S(2)}) collective-permute-start(bf16[128,1152]{1,0:T(8,128)(2,1)S(1)} %collective-permute-done.6.feats_y), channel_id=1, source_target_pairs={{0,1},{1,0},{2,3},{3,2},{4,5},{5,4},{6,7},{7,6},{8,9},{9,8},{10,11... | collective-permute-start | bytes 884744 | tf_op jit(solution)/shard_map/ppermute | solution.py:288
  61.7 4.4 %collective-permute-start.5 = (bf16[128,1152]{1,0:T(8,128)(2,1)}, bf16[128,1152]{1,0:T(8,128)(2,1)S(1)}, u32[]{:S(2)}, u32[]{:S(2)}) collective-permute-start(bf16[128,1152]{1,0:T(8,128)(2,1)} %feats.4), channel_id=1, source_target_pairs={{0,1},{1,0},{2,3},{3,2},{4,5},{5,4},{6,7},{7,6},{8,9},{9,8},{10,11... | collective-permute-start | bytes 884744 | tf_op jit(solution)/shard_map/ppermute | solution.py:287
  63.7 10.1 %collective-permute-start.8 = (bf16[136,1152]{1,0:T(8,128)(2,1)S(1)}, bf16[136,1152]{1,0:T(8,128)(2,1)S(1)}, u32[]{:S(2)}, u32[]{:S(2)}) collective-permute-start(bf16[136,1152]{1,0:T(8,128)(2,1)S(1)} %collective-permute-done.2.txt_b), channel_id=1, source_target_pairs={{0,1},{1,2},{2,3},{3,4},{4,5},{5,6},{6,7},{7,8},{8,9},{9,10},{10,1... | collective-permute-start | bytes 940040 | tf_op jit(solution)/shard_map/ppermute | solution.py:23
  89.8 24.1 %all-to-all-start.2 = ((bf16[48,16,128]{2,1,0:T(8,128)(2,1)}), bf16[48,16,128]{2,1,0:T(8,128)(2,1)S(1)}, u32[]{:S(2)}, u32[]{:S(2)}) async-start(bf16[48,16,128]{2,1,0:T(8,128)(2,1)} %shard_map.97), calls=%async_computation.2 | async-start | bytes 393216 | tf_op jit(solution)/shard_map/all_to_all | solution.py:314
  97.4 1.8 %copy-start.4 = (bf16[1152,1152]{1,0:T(8,128)(2,1)S(1)}, bf16[1152,1152]{1,0:T(8,128)(2,1)}, u32[]{:S(2)}) copy-start(bf16[1152,1152]{1,0:T(8,128)(2,1)} %head.3) | copy-start | bytes 7962628

commit v2 on v1

--- a/solution.py
+++ b/solution.py
@@ -23,7 +23,7 @@
     return lax.ppermute(value, axes, [(i, (i + by) % length) for i in range(length)])
 
 
-def kernel_call(kernel, out_shape, flops, scalars, arrays, scratch=()):
+def kernel_call(kernel, out_shape, flops, scalars, arrays, scratch=(), vmem=VMEM_BYTES):
     moved = sum(v.size * v.dtype.itemsize for v in arrays)
     moved += sum(v.size * v.dtype.itemsize for v in jax.tree.leaves(out_shape))
     return pl.pallas_call(
@@ -33,7 +33,7 @@
         + [pl.BlockSpec(memory_space=pltpu.VMEM)] * len(arrays),
         out_specs=jax.tree.map(lambda _: pl.BlockSpec(memory_space=pltpu.VMEM), out_shape),
         scratch_shapes=scratch,
-        compiler_params=pltpu.CompilerParams(vmem_limit_bytes=VMEM_BYTES),
+        compiler_params=pltpu.CompilerParams(vmem_limit_bytes=vmem),
         cost_estimate=pl.CostEstimate(flops=flops, bytes_accessed=moved, transcendentals=0),
     )(*scalars, *arrays)
 
@@ -145,48 +145,40 @@
                 turned[(yl * N_CORE + core) * N_X + x] = columns[at : at + part].astype(BF16)
 
 
+def image_pairs(scale, bias, image, own_code, texts, code, apart, total):
+    match = met_pairs(own_code, code, apart, total)
+    value = signed_logit(dot_nt(image, texts), match, scale, bias)
+    loss = jnp.sum(softplus(value), axis=-1, keepdims=True)
+    return jnp.dot(slope_of(value, match), texts, preferred_element_type=F32), loss
+
+
+def text_rows(feats, head):
+    pre = jnp.dot(feats, head[...], preferred_element_type=F32)
+    return (pre / lengths_of(pre)).astype(BF16)
+
+
 def image_side_kernel(
-    scale_log,
-    logit_bias,
-    img,
-    unit,
-    txt,
-    txt_g,
-    txt_b,
-    txt_bg,
-    turned,
-    head,
-    grad_out,
-    loss_out,
-    text_out,
+    scale_log, logit_bias, img, unit, txt, txt_g, txt_b, turned, head, grad_out, loss_out, text_out
 ):
     scale = jnp.exp(jnp.full((1, 1), scale_log[0], F32))
     bias = logit_bias[0]
     b, g, n_blk, n_group = homes()
     last_b = b - lax.rem(b + n_blk - 1, n_blk)
     last_g = g - lax.rem(g + n_group - 1, n_group)
-    aparts = (0 * b, last_g, last_b * n_group, last_b * n_group + last_g)
-    wide = img[...].astype(F32)
-    size = lengths_of(wide)
-    own = wide / size
-    image = own.astype(BF16)
-    total = jnp.zeros(wide.shape, F32)
-    loss = jnp.zeros((wide.shape[0], 1), F32)
-    own_code = split_block(txt)[1]
-    for block, apart in zip((txt, txt_g, txt_b, txt_bg), aparts):
+    image, _ = split_block(img)
+    _, own_code = split_block(txt)
+    grad, loss = image_pairs(
+        scale, bias, image, own_code, unit[...].astype(BF16), own_code, 0 * b, n_blk * n_group
+    )
+    for block, apart in ((txt_g, last_g), (txt_b, last_b * n_group)):
         feats, code = split_block(block)
-        if block is txt:
-            texts = unit[...].astype(BF16)
-        else:
-            pre = jnp.dot(feats, head[...], preferred_element_type=F32)
-            texts = (pre / lengths_of(pre)).astype(BF16)
-        match = met_pairs(own_code, code, apart, n_blk * n_group)
-        value = signed_logit(dot_nt(image, texts), match, scale, bias)
-        loss += jnp.sum(softplus(value), axis=-1, keepdims=True)
-        total += jnp.dot(slope_of(value, match), texts, preferred_element_type=F32)
-    grad = scale * total
-    grad_out[...] = (grad - own * jnp.sum(own * grad, axis=-1, keepdims=True)) / size
-    loss_out[...] = jnp.broadcast_to(loss, (loss.shape[0], loss.shape[0])).T[0:1]
+        more, lost = image_pairs(
+            scale, bias, image, own_code, text_rows(feats, head), code, apart, n_blk * n_group
+        )
+        grad += more
+        loss += lost
+    grad_out[...] = grad
+    loss_out[...] = loss
     blocks = [
         turned[(yl * N_CORE + core) * N_X + x].astype(F32)
         for yl in range(N_YL)
@@ -195,6 +187,30 @@
     ]
     delta = jnp.concatenate(blocks, axis=0).T.astype(BF16)
     text_out[...] = dot_nt(delta, head[...])
+
+
+def diagonal_kernel(
+    scale_log, logit_bias, raw, img, txt, txt_bg, head, grad_in, loss_in, grad_out, loss_out
+):
+    scale = jnp.exp(jnp.full((1, 1), scale_log[0], F32))
+    bias = logit_bias[0]
+    b, g, n_blk, n_group = homes()
+    last_b = b - lax.rem(b + n_blk - 1, n_blk)
+    last_g = g - lax.rem(g + n_group - 1, n_group)
+    image, _ = split_block(img)
+    _, own_code = split_block(txt)
+    feats, code = split_block(txt_bg)
+    apart = last_b * n_group + last_g
+    more, lost = image_pairs(
+        scale, bias, image, own_code, text_rows(feats, head), code, apart, n_blk * n_group
+    )
+    grad = scale * (grad_in[...] + more)
+    wide = raw[...].astype(F32)
+    size = lengths_of(wide)
+    own = wide / size
+    grad_out[...] = (grad - own * jnp.sum(own * grad, axis=-1, keepdims=True)) / size
+    loss = loss_in[...] + lost
+    loss_out[...] = jnp.broadcast_to(loss, (loss.shape[0], loss.shape[0])).T[0:1]
 
 
 def head_kernel(place, met, feats, feats_c, feats_y, feats_cy, out):
@@ -257,21 +273,25 @@
     score = 2 * rows * rows * width
 
     block = like((rows + 8, width), BF16)
-    img, txt = kernel_call(block_kernel, (block, block), 0, (), (image_emb, text_feats, ids))
+    img, txt = kernel_call(
+        block_kernel, (block, block), 0, (), (image_emb, text_feats, ids), vmem=60 * 1024 * 1024
+    )
     img_b = shifted(img, BLK, -1)
     txt_b = shifted(txt, BLK, 1)
-    img_g = shifted(img, GROUP, -1)
-    txt_g = shifted(after(txt, img_g), GROUP, 1)
+    swap = [(0, 1), (1, 0)]
     unit, length = kernel_call(
         text_kernel,
         (like((rows, width), F32), like((rows, 1), F32)),
         TEXT_FLOPS,
         (),
-        (after(text_feats, img_g), text_head),
-    )
-    img_b, txt_b = lax.optimization_barrier((img_b, txt_b, unit, txt_g))[:2]
+        (after(text_feats, img), text_head),
+    )
+    late_img, late_txt, late_feats = lax.optimization_barrier((img, txt, text_feats, unit))[:3]
+    img_g = shifted(late_img, GROUP, -1)
+    txt_g = shifted(late_txt, GROUP, 1)
+    feats_c = lax.ppermute(late_feats, "core", swap)
+    img_b, txt_b = lax.optimization_barrier((img_b, txt_b, unit, feats_c))[:2]
     img_bg = shifted(img_b, GROUP, -1)
-    swap = [(0, 1), (1, 0)]
     feats_y = lax.ppermute(after(text_feats, img_b), "yl", swap)
 
     part = width // (N_YL * N_X * N_CORE)
@@ -280,24 +300,28 @@
         like((N_YL * N_CORE * N_X, part, rows), BF16),
         8 * score,
         (scale_log, logit_bias),
-        (unit, length, img, img_g, img_b, img_bg),
-    )
-
-    late_txt, late_b = lax.optimization_barrier((text_feats, txt_b, turned))[:2]
-    feats_c = lax.ppermute(late_txt, "core", swap)
+        (after(unit, txt_g), length, img, img_g, img_b, img_bg),
+    )
+
     feats_cy = lax.ppermute(feats_y, "core", swap)
-    txt_bg = shifted(late_b, GROUP, 1)
     place = lax.axis_index(QUAD).reshape(1)
     quads = turned.reshape(N_YL * N_CORE, N_X, part, rows)
     met = lax.all_to_all(quads, QUAD, 0, 0)
-    partial = kernel_call(
+    products = kernel_call(
         head_kernel,
         like((N_X, part, width), BF16),
         2 * 4 * rows * width * N_X * part,
         (place,),
         (met, text_feats, feats_c, feats_y, feats_cy),
     )
-    partial = lax.all_to_all(after(partial, txt_bg), "x", 0, 0)
+    partial = lax.all_to_all(products, "x", 0, 0)
+    part_grad, part_loss, text_grad = kernel_call(
+        image_side_kernel,
+        (like((rows, width), F32), like((rows, 1), F32), like((rows, width), F32)),
+        24 * score + 24 * rows * width * width,
+        (scale_log, logit_bias),
+        (after(img, products), unit, txt, txt_g, txt_b, turned, text_head),
+    )
     depth = width // n_blk
     packed = kernel_call(
         pack_kernel,
@@ -311,24 +335,17 @@
             pltpu.VMEM((n_blk, 16, 128), F32),
         ),
     )
+    packed = after(packed, part_loss)
     summed = lax.all_to_all(packed, BLK, 0, 0)
+    txt_bg = shifted(after(txt_b, packed), GROUP, 1)
     head_grad = kernel_call(unpack_kernel, like((depth, part), F32), 0, (), (summed,))
 
-    image_grad, row_loss, text_grad = kernel_call(
-        image_side_kernel,
-        (like((rows, width), F32), like((1, rows), F32), like((rows, width), F32)),
-        8 * score + 8 * rows * width * width,
+    image_grad, row_loss = kernel_call(
+        diagonal_kernel,
+        (like((rows, width), F32), like((1, rows), F32)),
+        12 * score + 12 * rows * width * width,
         (scale_log, logit_bias),
-        (
-            after(image_emb, packed),
-            unit,
-            txt,
-            txt_g,
-            txt_b,
-            txt_bg,
-            turned,
-            text_head,
-        ),
+        (image_emb, img, txt, txt_bg, text_head, part_grad, part_loss),
     )
     return (image_grad, text_grad, head_grad, row_loss.reshape(rows))
 

time: 115 us -> 105 us (0.913)
  the two profiles are of different devices: /device:TPU:2 before, /device:TPU:16 now
where the time goes in v2:
time: 105 us; the launch traced here: 104 us
  starting transfers between devices  52.4 us (50%)
  waiting for transfers between devices  24 us (23%)
  Pallas kernels  18 us (17%)
  local copies, waits for them, and re-layouts  7.13 us (7%)
  between operations  2.1 us (2%)
    ppermute x6, starting transfers between devices, shifted(): lax.ppermute(value, axes, [(i, (i + by) % length) for i in range(length)])  28.7 us
    pallas_call x8, Pallas kernels, kernel_call(): pl.pallas_call(kernel, out_shape=out_shape, in_specs=[pl.BlockSpec(memory...  18 us
    ppermute x6, waiting for transfers between devices, shifted(): lax.ppermute(value, axes, [(i, (i + by) % length) for i in range(length)])  15.8 us
    all_to_all x1, starting transfers between devices, body(): summed = lax.all_to_all(packed, BLK, 0, 0)  8.76 us
    unnamed x16, local copies, waits for them, and re-layouts  7.13 us
    all_to_all x1, starting transfers between devices, body(): partial = lax.all_to_all(products, 'x', 0, 0)  4.16 us
    all_to_all x1, starting transfers between devices, body(): met = lax.all_to_all(quads, QUAD, 0, 0)  3.76 us
    all_to_all x1, waiting for transfers between devices, body(): partial = lax.all_to_all(products, 'x', 0, 0)  3.37 us
  transfers between devices with their start and end apart: 12, of which 7 were waited for; matrix products, arithmetic and copies ran while one was open for 0% of the time, Pallas kernels for 11%

profile of v2, /device:TPU:16, one launch (start us, length us, event | category | flops | bytes accessed | tf_op | source)
XLA Modules:
  0.0 103.7 jit_solution(11223054676042563441)
XLA Ops:
  0.6 2.0 %shard_map.93 = (bf16[136,1152]{1,0:T(8,128)(2,1)}, bf16[136,1152]{1,0:T(8,128)(2,1)}) custom-call(bf16[128,1152]{1,0:T(8,128)(2,1)} %raw.1, bf16[128,1152]{1,0:T(8,128)(2,1)} %feats.4, s32[1,128]{1,0:T(1,128)} %bitcast.4), custom_call_target="tpu_custom_call" | custom-call | bytes 1217024 | tf_op jit(solution)/shard_map/pallas_call | solution.py:29
  2.6 14.3 %collective-permute-start = (bf16[136,1152]{1,0:T(8,128)(2,1)}, bf16[136,1152]{1,0:T(8,128)(2,1)S(1)}, u32[]{:S(2)}, u32[]{:S(2)}) collective-permute-start(bf16[136,1152]{1,0:T(8,128)(2,1)} %get-tuple-element.36.img), channel_id=1, source_target_pairs={{0,752},{16,0},{32,16},{48,32},{64,48},{80,64},{96,80},{112,96},{1... | collective-permute-start | bytes 940040 | tf_op jit(solution)/shard_map/ppermute | solution.py:23
  17.0 0.0 copy-start
  17.0 2.1 %collective-permute-start.1 = (bf16[136,1152]{1,0:T(8,128)(2,1)}, bf16[136,1152]{1,0:T(8,128)(2,1)S(1)}, u32[]{:S(2)}, u32[]{:S(2)}) collective-permute-start(bf16[136,1152]{1,0:T(8,128)(2,1)} %get-tuple-element.30.txt), channel_id=1, source_target_pairs={{0,16},{16,32},{32,48},{48,64},{64,80},{80,96},{96,112},{112,128},... | collective-permute-start | bytes 940040 | tf_op jit(solution)/shard_map/ppermute | solution.py:23
  19.0 0.0 copy-start.2
  19.1 1.7 %copy-done.2 = bf16[1152,1152]{1,0:T(8,128)(2,1)S(1)} copy-done((bf16[1152,1152]{1,0:T(8,128)(2,1)S(1)}, bf16[1152,1152]{1,0:T(8,128)(2,1)}, u32[]{:S(2)}) %copy-start.2) | copy-done | bytes 2654232
  20.8 0.0 copy-start.5
  20.8 1.7 %shard_map.94 = (f32[128,1152]{1,0:T(8,128)S(1)}, f32[128,1]{1,0:T(8,128)S(1)}) custom-call(bf16[128,1152]{1,0:T(8,128)(2,1)} %feats.4, bf16[1152,1152]{1,0:T(8,128)(2,1)S(1)} %copy-done.2), custom_call_target="tpu_custom_call" | custom-call | flops 12000000000 | bytes 3539456 | tf_op jit(solution)/shard_map/pallas_call | solution.py:29
  22.5 1.9 %collective-permute-start.2 = (bf16[128,1152]{1,0:T(8,128)(2,1)}, bf16[128,1152]{1,0:T(8,128)(2,1)S(1)}, u32[]{:S(2)}, u32[]{:S(2)}) collective-permute-start(bf16[128,1152]{1,0:T(8,128)(2,1)} %feats.4), channel_id=1, source_target_pairs={{0,1},{1,0},{2,3},{3,2},{4,5},{5,4},{6,7},{7,6},{8,9},{9,8},{10,11... | collective-permute-start | bytes 884744 | tf_op jit(solution)/shard_map/ppermute | solution.py:292
  24.5 0.0 copy-done.5
  24.5 2.4 %collective-permute-start.3 = (bf16[136,1152]{1,0:T(8,128)(2,1)S(1)}, bf16[136,1152]{1,0:T(8,128)(2,1)S(1)}, u32[]{:S(2)}, u32[]{:S(2)}) collective-permute-start(bf16[136,1152]{1,0:T(8,128)(2,1)S(1)} %copy-done.5), channel_id=1, source_target_pairs={{0,1},{1,2},{2,3},{3,4},{4,5},{5,6},{6,7},{7,8},{8,9},{9,10},{10,1... | collective-permute-start | bytes 940040 | tf_op jit(solution)/shard_map/ppermute | solution.py:23
  26.9 0.0 copy-done
  26.9 5.3 %collective-permute-start.4 = (bf16[136,1152]{1,0:T(8,128)(2,1)S(1)}, bf16[136,1152]{1,0:T(8,128)(2,1)S(1)}, u32[]{:S(2)}, u32[]{:S(2)}) collective-permute-start(bf16[136,1152]{1,0:T(8,128)(2,1)S(1)} %copy-done), channel_id=1, source_target_pairs={{0,15},{1,0},{2,1},{3,2},{4,3},{5,4},{6,5},{7,6},{8,7},{9,8},{10,9... | collective-permute-start | bytes 940040 | tf_op jit(solution)/shard_map/ppermute | solution.py:23
  32.2 0.0 collective-permute-done.2.feats_c
  32.2 0.0 collective-permute-done.img_b
  32.2 5.6 %collective-permute-done.1.txt_b = bf16[136,1152]{1,0:T(8,128)(2,1)S(1)} collective-permute-done((bf16[136,1152]{1,0:T(8,128)(2,1)}, bf16[136,1152]{1,0:T(8,128)(2,1)S(1)}, u32[]{:S(2)}, u32[]{:S(2)}) %collective-permute-start.1) | collective-permute-done | bytes 313376 | tf_op jit(solution)/shard_map/ppermute | solution.py:23
  37.8 2.7 %collective-permute-start.5 = (bf16[136,1152]{1,0:T(8,128)(2,1)S(1)}, bf16[136,1152]{1,0:T(8,128)(2,1)S(1)}, u32[]{:S(2)}, u32[]{:S(2)}) collective-permute-start(bf16[136,1152]{1,0:T(8,128)(2,1)S(1)} %collective-permute-done.img_b), channel_id=1, source_target_pairs={{0,15},{1,0},{2,1},{3,2},{4,3},{5,4},{6,5},{7,6},{8,7},{9,8},{10,9... | collective-permute-start | bytes 940040 | tf_op jit(solution)/shard_map/ppermute | solution.py:23
  40.5 3.2 %collective-permute-start.6 = (bf16[128,1152]{1,0:T(8,128)(2,1)}, bf16[128,1152]{1,0:T(8,128)(2,1)S(1)}, u32[]{:S(2)}, u32[]{:S(2)}) collective-permute-start(bf16[128,1152]{1,0:T(8,128)(2,1)} %feats.4), channel_id=1, source_target_pairs={{0,8},{8,0},{1,9},{9,1},{2,10},{10,2},{3,11},{11,3},{4,12},{12,4},... | collective-permute-start | bytes 884744 | tf_op jit(solution)/shard_map/ppermute | solution.py:295
  45.0 0.0 collective-permute-done.3.txt_g
  45.0 0.0 collective-permute-done.4.img_g
  45.0 0.2 collective-permute-done.5.img_bg
  45.2 2.3 %shard_map.95.turned = bf16[16,72,128]{2,1,0:T(8,128)(2,1)} custom-call(f32[1]{0:T(128)S(6)} %copy.10.scale_log, f32[1]{0:T(128)S(6)} %copy.11.logit_bias, f32[128,1152]{1,0:T(8,128)S(1)} %get-tuple-element.31.unit, f32[128,1]{1,0:T(8,128)S(1)} %get-tuple-element.32.length, bf16[136,1152]{1,0:T(8,128)(2,1)S(1)} %copy-done, ...), custom_call_target="tpu_custom_call" | custom-call | flops 301989888 | bytes 2138624 | tf_op jit(solution)/shard_map/pallas_call | solution.py:29
  47.5 3.8 %all-to-all-start = ((bf16[4,4,72,128]{3,2,1,0:T(8,128)(2,1)}), bf16[4,4,72,128]{3,2,1,0:T(8,128)(2,1)S(1)}, u32[]{:S(2)}, u32[]{:S(2)}) async-start(bf16[4,4,72,128]{3,2,1,0:T(8,128)(2,1)} %bitcast.2), calls=%async_computation | async-start | bytes 589824 | tf_op jit(solution)/shard_map/all_to_all | solution.py:309
  51.3 1.7 %collective-permute-done.6.feats_y = bf16[128,1152]{1,0:T(8,128)(2,1)S(1)} collective-permute-done((bf16[128,1152]{1,0:T(8,128)(2,1)}, bf16[128,1152]{1,0:T(8,128)(2,1)S(1)}, u32[]{:S(2)}, u32[]{:S(2)}) %collective-permute-start.6) | collective-permute-done | bytes 294944 | tf_op jit(solution)/shard_map/ppermute | solution.py:295
  53.0 1.9 %collective-permute-start.7 = (bf16[128,1152]{1,0:T(8,128)(2,1)S(1)}, bf16[128,1152]{1,0:T(8,128)(2,1)S(1)}, u32[]{:S(2)}, u32[]{:S(2)}) collective-permute-start(bf16[128,1152]{1,0:T(8,128)(2,1)S(1)} %collective-permute-done.6.feats_y), channel_id=1, source_target_pairs={{0,1},{1,0},{2,3},{3,2},{4,5},{5,4},{6,7},{7,6},{8,9},{9,8},{10,11... | collective-permute-start | bytes 884744 | tf_op jit(solution)/shard_map/ppermute | solution.py:306
  54.9 1.5 %collective-permute-done.7.feats_cy = bf16[128,1152]{1,0:T(8,128)(2,1)S(1)} collective-permute-done((bf16[128,1152]{1,0:T(8,128)(2,1)S(1)}, bf16[128,1152]{1,0:T(8,128)(2,1)S(1)}, u32[]{:S(2)}, u32[]{:S(2)}) %collective-permute-start.7) | collective-permute-done | bytes 294944 | tf_op jit(solution)/shard_map/ppermute | solution.py:306
  56.4 1.6 %all-to-all-done.met = bf16[4,4,72,128]{3,2,1,0:T(8,128)(2,1)S(1)} async-done(((bf16[4,4,72,128]{3,2,1,0:T(8,128)(2,1)}), bf16[4,4,72,128]{3,2,1,0:T(8,128)(2,1)S(1)}, u32[]{:S(2)}, u32[]{:S(2)}) %all-to-all-start) | async-done | bytes 294944 | tf_op jit(solution)/shard_map/all_to_all | solution.py:309
  58.1 2.6 %shard_map.96 = bf16[4,72,1152]{2,1,0:T(8,128)(2,1)} custom-call(s32[1]{0:T(128)} %bitcast.1.place, bf16[4,4,72,128]{3,2,1,0:T(8,128)(2,1)S(1)} %all-to-all-done.met, bf16[128,1152]{1,0:T(8,128)(2,1)} %feats.4, bf16[128,1152]{1,0:T(8,128)(2,1)S(1)} %collective-permute-done.2.feats_c, bf16[128,1152]{1,0:T(8,128)(2,1)S(1)} %collective-permute-done.6.feats_y, ...), custom_call_target="tpu_custom_call" | custom-call | flops 339738624 | bytes 2138112 | tf_op jit(solution)/shard_map/pallas_call | solution.py:29
  60.7 4.2 %all-to-all-start.1 = ((bf16[4,72,1152]{2,1,0:T(8,128)(2,1)}), bf16[4,72,1152]{2,1,0:T(8,128)(2,1)S(1)}, u32[]{:S(2)}, u32[]{:S(2)}) async-start(bf16[4,72,1152]{2,1,0:T(8,128)(2,1)} %shard_map.96), calls=%async_computation.1 | async-start | bytes 1327104 | tf_op jit(solution)/shard_map/all_to_all | solution.py:317
  64.9 0.0 copy-start.3
  64.9 1.7 %copy-done.3 = bf16[1152,1152]{1,0:T(8,128)(2,1)S(1)} copy-done((bf16[1152,1152]{1,0:T(8,128)(2,1)S(1)}, bf16[1152,1152]{1,0:T(8,128)(2,1)}, u32[]{:S(2)}) %copy-start.3) | copy-done | bytes 2654232
  66.6 0.0 copy-start.1
  66.6 5.1 %shard_map.98 = (f32[128,1152]{1,0:T(8,128)S(1)}, f32[128,1]{1,0:T(8,128)S(1)}, f32[128,1152]{1,0:T(8,128)}) custom-call(f32[1]{0:T(128)S(6)} %copy.10.scale_log, f32[1]{0:T(128)S(6)} %copy.11.logit_bias, bf16[136,1152]{1,0:T(8,128)(2,1)S(1)} %copy-done, f32[128,1152]{1,0:T(8,128)S(1)} %get-tuple-element.31.unit, bf16[136,1152]{1,0:T(8,128)(2,1)S(1)} %copy-done.5, ...), custom_call_target="tpu_custom_call" | custom-call | flops 4982833152 | bytes 5972480 | tf_op jit(solution)/shard_map/pallas_call | solution.py:29
  71.8 0.0 copy-start.6
  71.8 0.8 copy-done.6
  72.6 3.4 %all-to-all-done.1.parts = bf16[4,72,1152]{2,1,0:T(8,128)(2,1)S(1)} async-done(((bf16[4,72,1152]{2,1,0:T(8,128)(2,1)}), bf16[4,72,1152]{2,1,0:T(8,128)(2,1)S(1)}, u32[]{:S(2)}, u32[]{:S(2)}) %all-to-all-start.1) | async-done | bytes 663584 | tf_op jit(solution)/shard_map/all_to_all | solution.py:317
  76.0 1.2 %shard_map.97 = bf16[48,16,128]{2,1,0:T(8,128)(2,1)} custom-call(bf16[4,72,1152]{2,1,0:T(8,128)(2,1)S(1)} %all-to-all-done.1.parts), custom_call_target="tpu_custom_call" | custom-call | bytes 860160 | tf_op jit(solution)/shard_map/pallas_call | solution.py:29
  77.1 8.8 %all-to-all-start.2 = ((bf16[48,16,128]{2,1,0:T(8,128)(2,1)}), bf16[48,16,128]{2,1,0:T(8,128)(2,1)S(1)}, u32[]{:S(2)}, u32[]{:S(2)}) async-start(bf16[48,16,128]{2,1,0:T(8,128)(2,1)} %shard_map.97), calls=%async_computation.2 | async-start | bytes 393216 | tf_op jit(solution)/shard_map/all_to_all | solution.py:339
  85.9 1.9 %collective-permute-start.8 = (bf16[136,1152]{1,0:T(8,128)(2,1)S(1)}, bf16[136,1152]{1,0:T(8,128)(2,1)S(1)}, u32[]{:S(2)}, u32[]{:S(2)}) collective-permute-start(bf16[136,1152]{1,0:T(8,128)(2,1)S(1)} %collective-permute-done.1.txt_b), channel_id=1, source_target_pairs={{0,1},{1,2},{2,3},{3,4},{4,5},{5,6},{6,7},{7,8},{8,9},{9,10},{10,1... | collective-permute-start | bytes 940040 | tf_op jit(solution)/shard_map/ppermute | solution.py:23
  87.8 10.0 %collective-permute-done.8.txt_bg = bf16[136,1152]{1,0:T(8,128)(2,1)S(1)} collective-permute-done((bf16[136,1152]{1,0:T(8,128)(2,1)S(1)}, bf16[136,1152]{1,0:T(8,128)(2,1)S(1)}, u32[]{:S(2)}, u32[]{:S(2)}) %collective-permute-start.8) | collective-permute-done | bytes 313376 | tf_op jit(solution)/shard_map/ppermute | solution.py:23
  97.9 0.0 copy-done.1
  97.9 0.0 copy-start.4
  97.9 1.7 %copy-done.4 = bf16[1152,1152]{1,0:T(8,128)(2,1)S(1)} copy-done((bf16[1152,1152]{1,0:T(8,128)(2,1)S(1)}, bf16[1152,1152]{1,0:T(8,128)(2,1)}, u32[]{:S(2)}) %copy-start.4) | copy-done | bytes 2654232
  99.6 0.0 copy-start.7
  99.6 1.1 %copy-done.7 = f32[128,1152]{1,0:T(8,128)S(1)} copy-done((f32[128,1152]{1,0:T(8,128)S(1)}, f32[128,1152]{1,0:T(8,128)}, u32[]{:S(2)}) %copy-start.7) | copy-done | bytes 589848
  100.7 2.3 %shard_map.99 = (f32[128,1152]{1,0:T(8,128)}, f32[1,128]{1,0:T(1,128)}) custom-call(f32[1]{0:T(128)S(6)} %copy.10.scale_log, f32[1]{0:T(128)S(6)} %copy.11.logit_bias, bf16[128,1152]{1,0:T(8,128)(2,1)S(1)} %copy-done.1, bf16[136,1152]{1,0:T(8,128)(2,1)S(1)} %copy-done, bf16[136,1152]{1,0:T(8,128)(2,1)S(1)} %copy-done.5, ...), custom_call_target="tpu_custom_call" | custom-call | flops 2491416576 | bytes 5069824 | tf_op jit(solution)/shard_map/pallas_call | solution.py:29
  103.0 0.0 all-to-all-done.2.parts
  103.0 0.7 shard_map.100
Async XLA Ops:
  2.6 29.6 %collective-permute-start = (bf16[136,1152]{1,0:T(8,128)(2,1)}, bf16[136,1152]{1,0:T(8,128)(2,1)S(1)}, u32[]{:S(2)}, u32[]{:S(2)}) collective-permute-start(bf16[136,1152]{1,0:T(8,128)(2,1)} %get-tuple-element.36.img), channel_id=1, source_target_pairs={{0,752},{16,0},{32,16},{48,32},{64,48},{80,64},{96,80},{112,96},{1... | collective-permute-start | bytes 940040 | tf_op jit(solution)/shard_map/ppermute | solution.py:23
  17.0 9.9 %copy-start = (bf16[136,1152]{1,0:T(8,128)(2,1)S(1)}, bf16[136,1152]{1,0:T(8,128)(2,1)}, u32[]{:S(2)}) copy-start(bf16[136,1152]{1,0:T(8,128)(2,1)} %get-tuple-element.36.img) | copy-start | bytes 940036
  17.0 20.8 %collective-permute-start.1 = (bf16[136,1152]{1,0:T(8,128)(2,1)}, bf16[136,1152]{1,0:T(8,128)(2,1)S(1)}, u32[]{:S(2)}, u32[]{:S(2)}) collective-permute-start(bf16[136,1152]{1,0:T(8,128)(2,1)} %get-tuple-element.30.txt), channel_id=1, source_target_pairs={{0,16},{16,32},{32,48},{48,64},{64,80},{80,96},{96,112},{112,128},... | collective-permute-start | bytes 940040 | tf_op jit(solution)/shard_map/ppermute | solution.py:23
  19.0 1.8 %copy-start.2 = (bf16[1152,1152]{1,0:T(8,128)(2,1)S(1)}, bf16[1152,1152]{1,0:T(8,128)(2,1)}, u32[]{:S(2)}) copy-start(bf16[1152,1152]{1,0:T(8,128)(2,1)} %head.5) | copy-start | bytes 7962628
  20.8 3.7 %copy-start.5 = (bf16[136,1152]{1,0:T(8,128)(2,1)S(1)}, bf16[136,1152]{1,0:T(8,128)(2,1)}, u32[]{:S(2)}) copy-start(bf16[136,1152]{1,0:T(8,128)(2,1)} %get-tuple-element.30.txt) | copy-start | bytes 940036
  22.5 9.7 %collective-permute-start.2 = (bf16[128,1152]{1,0:T(8,128)(2,1)}, bf16[128,1152]{1,0:T(8,128)(2,1)S(1)}, u32[]{:S(2)}, u32[]{:S(2)}) collective-permute-start(bf16[128,1152]{1,0:T(8,128)(2,1)} %feats.4), channel_id=1, source_target_pairs={{0,1},{1,0},{2,3},{3,2},{4,5},{5,4},{6,7},{7,6},{8,9},{9,8},{10,11... | collective-permute-start | bytes 884744 | tf_op jit(solution)/shard_map/ppermute | solution.py:292
  24.5 20.5 %collective-permute-start.3 = (bf16[136,1152]{1,0:T(8,128)(2,1)S(1)}, bf16[136,1152]{1,0:T(8,128)(2,1)S(1)}, u32[]{:S(2)}, u32[]{:S(2)}) collective-permute-start(bf16[136,1152]{1,0:T(8,128)(2,1)S(1)} %copy-done.5), channel_id=1, source_target_pairs={{0,1},{1,2},{2,3},{3,4},{4,5},{5,6},{6,7},{7,8},{8,9},{9,10},{10,1... | collective-permute-start | bytes 940040 | tf_op jit(solution)/shard_map/ppermute | solution.py:23
  26.9 18.1 %collective-permute-start.4 = (bf16[136,1152]{1,0:T(8,128)(2,1)S(1)}, bf16[136,1152]{1,0:T(8,128)(2,1)S(1)}, u32[]{:S(2)}, u32[]{:S(2)}) collective-permute-start(bf16[136,1152]{1,0:T(8,128)(2,1)S(1)} %copy-done), channel_id=1, source_target_pairs={{0,15},{1,0},{2,1},{3,2},{4,3},{5,4},{6,5},{7,6},{8,7},{9,8},{10,9... | collective-permute-start | bytes 940040 | tf_op jit(solution)/shard_map/ppermute | solution.py:23
  37.8 7.4 %collective-permute-start.5 = (bf16[136,1152]{1,0:T(8,128)(2,1)S(1)}, bf16[136,1152]{1,0:T(8,128)(2,1)S(1)}, u32[]{:S(2)}, u32[]{:S(2)}) collective-permute-start(bf16[136,1152]{1,0:T(8,128)(2,1)S(1)} %collective-permute-done.img_b), channel_id=1, source_target_pairs={{0,15},{1,0},{2,1},{3,2},{4,3},{5,4},{6,5},{7,6},{8,7},{9,8},{10,9... | collective-permute-start | bytes 940040 | tf_op jit(solution)/shard_map/ppermute | solution.py:23
  40.5 12.5 %collective-permute-start.6 = (bf16[128,1152]{1,0:T(8,128)(2,1)}, bf16[128,1152]{1,0:T(8,128)(2,1)S(1)}, u32[]{:S(2)}, u32[]{:S(2)}) collective-permute-start(bf16[128,1152]{1,0:T(8,128)(2,1)} %feats.4), channel_id=1, source_target_pairs={{0,8},{8,0},{1,9},{9,1},{2,10},{10,2},{3,11},{11,3},{4,12},{12,4},... | collective-permute-start | bytes 884744 | tf_op jit(solution)/shard_map/ppermute | solution.py:295
  47.5 10.5 %all-to-all-start = ((bf16[4,4,72,128]{3,2,1,0:T(8,128)(2,1)}), bf16[4,4,72,128]{3,2,1,0:T(8,128)(2,1)S(1)}, u32[]{:S(2)}, u32[]{:S(2)}) async-start(bf16[4,4,72,128]{3,2,1,0:T(8,128)(2,1)} %bitcast.2), calls=%async_computation | async-start | bytes 589824 | tf_op jit(solution)/shard_map/all_to_all | solution.py:309
  53.0 3.5 %collective-permute-start.7 = (bf16[128,1152]{1,0:T(8,128)(2,1)S(1)}, bf16[128,1152]{1,0:T(8,128)(2,1)S(1)}, u32[]{:S(2)}, u32[]{:S(2)}) collective-permute-start(bf16[128,1152]{1,0:T(8,128)(2,1)S(1)} %collective-permute-done.6.feats_y), channel_id=1, source_target_pairs={{0,1},{1,0},{2,3},{3,2},{4,5},{5,4},{6,7},{7,6},{8,9},{9,8},{10,11... | collective-permute-start | bytes 884744 | tf_op jit(solution)/shard_map/ppermute | solution.py:306
  60.7 15.3 %all-to-all-start.1 = ((bf16[4,72,1152]{2,1,0:T(8,128)(2,1)}), bf16[4,72,1152]{2,1,0:T(8,128)(2,1)S(1)}, u32[]{:S(2)}, u32[]{:S(2)}) async-start(bf16[4,72,1152]{2,1,0:T(8,128)(2,1)} %shard_map.96), calls=%async_computation.1 | async-start | bytes 1327104 | tf_op jit(solution)/shard_map/all_to_all | solution.py:317
  64.9 1.7 %copy-start.3 = (bf16[1152,1152]{1,0:T(8,128)(2,1)S(1)}, bf16[1152,1152]{1,0:T(8,128)(2,1)}, u32[]{:S(2)}) copy-start(bf16[1152,1152]{1,0:T(8,128)(2,1)} %head.5) | copy-start | bytes 7962628
  66.6 31.3 %copy-start.1 = (bf16[128,1152]{1,0:T(8,128)(2,1)S(1)}, bf16[128,1152]{1,0:T(8,128)(2,1)}, u32[]{:S(2)}) copy-start(bf16[128,1152]{1,0:T(8,128)(2,1)} %raw.1) | copy-start | bytes 884740
  71.8 0.8 copy-start.6
  77.1 25.8 %all-to-all-start.2 = ((bf16[48,16,128]{2,1,0:T(8,128)(2,1)}), bf16[48,16,128]{2,1,0:T(8,128)(2,1)S(1)}, u32[]{:S(2)}, u32[]{:S(2)}) async-start(bf16[48,16,128]{2,1,0:T(8,128)(2,1)} %shard_map.97), calls=%async_computation.2 | async-start | bytes 393216 | tf_op jit(solution)/shard_map/all_to_all | solution.py:339
  85.9 12.0 %collective-permute-start.8 = (bf16[136,1152]{1,0:T(8,128)(2,1)S(1)}, bf16[136,1152]{1,0:T(8,128)(2,1)S(1)}, u32[]{:S(2)}, u32[]{:S(2)}) collective-permute-start(bf16[136,1152]{1,0:T(8,128)(2,1)S(1)} %collective-permute-done.1.txt_b), channel_id=1, source_target_pairs={{0,1},{1,2},{2,3},{3,4},{4,5},{5,6},{6,7},{7,8},{8,9},{9,10},{10,1... | collective-permute-start | bytes 940040 | tf_op jit(solution)/shard_map/ppermute | solution.py:23
  97.9 1.8 %copy-start.4 = (bf16[1152,1152]{1,0:T(8,128)(2,1)S(1)}, bf16[1152,1152]{1,0:T(8,128)(2,1)}, u32[]{:S(2)}) copy-start(bf16[1152,1152]{1,0:T(8,128)(2,1)} %head.5) | copy-start | bytes 7962628
  99.6 1.1 %copy-start.7 = (f32[128,1152]{1,0:T(8,128)S(1)}, f32[128,1152]{1,0:T(8,128)}, u32[]{:S(2)}) copy-start(f32[128,1152]{1,0:T(8,128)} %copy-done.6) | copy-start | bytes 1769476

commit v3 on v1

--- a/solution.py
+++ b/solution.py
@@ -23,7 +23,7 @@
     return lax.ppermute(value, axes, [(i, (i + by) % length) for i in range(length)])
 
 
-def kernel_call(kernel, out_shape, flops, scalars, arrays, scratch=()):
+def kernel_call(kernel, out_shape, flops, scalars, arrays, scratch=(), vmem=VMEM_BYTES):
     moved = sum(v.size * v.dtype.itemsize for v in arrays)
     moved += sum(v.size * v.dtype.itemsize for v in jax.tree.leaves(out_shape))
     return pl.pallas_call(
@@ -33,7 +33,7 @@
         + [pl.BlockSpec(memory_space=pltpu.VMEM)] * len(arrays),
         out_specs=jax.tree.map(lambda _: pl.BlockSpec(memory_space=pltpu.VMEM), out_shape),
         scratch_shapes=scratch,
-        compiler_params=pltpu.CompilerParams(vmem_limit_bytes=VMEM_BYTES),
+        compiler_params=pltpu.CompilerParams(vmem_limit_bytes=vmem),
         cost_estimate=pl.CostEstimate(flops=flops, bytes_accessed=moved, transcendentals=0),
     )(*scalars, *arrays)
 
@@ -257,21 +257,25 @@
     score = 2 * rows * rows * width
 
     block = like((rows + 8, width), BF16)
-    img, txt = kernel_call(block_kernel, (block, block), 0, (), (image_emb, text_feats, ids))
+    img, txt = kernel_call(
+        block_kernel, (block, block), 0, (), (image_emb, text_feats, ids), vmem=60 * 1024 * 1024
+    )
     img_b = shifted(img, BLK, -1)
     txt_b = shifted(txt, BLK, 1)
-    img_g = shifted(img, GROUP, -1)
-    txt_g = shifted(after(txt, img_g), GROUP, 1)
+    swap = [(0, 1), (1, 0)]
     unit, length = kernel_call(
         text_kernel,
         (like((rows, width), F32), like((rows, 1), F32)),
         TEXT_FLOPS,
         (),
-        (after(text_feats, img_g), text_head),
-    )
-    img_b, txt_b = lax.optimization_barrier((img_b, txt_b, unit, txt_g))[:2]
+        (after(text_feats, img), text_head),
+    )
+    late_img, late_txt, late_feats = lax.optimization_barrier((img, txt, text_feats, unit))[:3]
+    img_g = shifted(late_img, GROUP, -1)
+    txt_g = shifted(late_txt, GROUP, 1)
+    feats_c = lax.ppermute(late_feats, "core", swap)
+    img_b, txt_b = lax.optimization_barrier((img_b, txt_b, unit, feats_c))[:2]
     img_bg = shifted(img_b, GROUP, -1)
-    swap = [(0, 1), (1, 0)]
     feats_y = lax.ppermute(after(text_feats, img_b), "yl", swap)
 
     part = width // (N_YL * N_X * N_CORE)
@@ -280,24 +284,39 @@
         like((N_YL * N_CORE * N_X, part, rows), BF16),
         8 * score,
         (scale_log, logit_bias),
-        (unit, length, img, img_g, img_b, img_bg),
-    )
-
-    late_txt, late_b = lax.optimization_barrier((text_feats, txt_b, turned))[:2]
-    feats_c = lax.ppermute(late_txt, "core", swap)
+        (after(unit, txt_g), length, img, img_g, img_b, img_bg),
+    )
+
+    late_b = after(txt_b, turned)
     feats_cy = lax.ppermute(feats_y, "core", swap)
     txt_bg = shifted(late_b, GROUP, 1)
     place = lax.axis_index(QUAD).reshape(1)
     quads = turned.reshape(N_YL * N_CORE, N_X, part, rows)
     met = lax.all_to_all(quads, QUAD, 0, 0)
-    partial = kernel_call(
+    products = kernel_call(
         head_kernel,
         like((N_X, part, width), BF16),
         2 * 4 * rows * width * N_X * part,
         (place,),
         (met, text_feats, feats_c, feats_y, feats_cy),
     )
-    partial = lax.all_to_all(after(partial, txt_bg), "x", 0, 0)
+    partial = lax.all_to_all(products, "x", 0, 0)
+    image_grad, row_loss, text_grad = kernel_call(
+        image_side_kernel,
+        (like((rows, width), F32), like((1, rows), F32), like((rows, width), F32)),
+        24 * score + 24 * rows * width * width,
+        (scale_log, logit_bias),
+        (
+            after(image_emb, products),
+            unit,
+            txt,
+            txt_g,
+            txt_b,
+            txt_bg,
+            turned,
+            text_head,
+        ),
+    )
     depth = width // n_blk
     packed = kernel_call(
         pack_kernel,
@@ -311,25 +330,10 @@
             pltpu.VMEM((n_blk, 16, 128), F32),
         ),
     )
+    packed = after(packed, row_loss)
     summed = lax.all_to_all(packed, BLK, 0, 0)
     head_grad = kernel_call(unpack_kernel, like((depth, part), F32), 0, (), (summed,))
 
-    image_grad, row_loss, text_grad = kernel_call(
-        image_side_kernel,
-        (like((rows, width), F32), like((1, rows), F32), like((rows, width), F32)),
-        8 * score + 8 * rows * width * width,
-        (scale_log, logit_bias),
-        (
-            after(image_emb, packed),
-            unit,
-            txt,
-            txt_g,
-            txt_b,
-            txt_bg,
-            turned,
-            text_head,
-        ),
-    )
     return (image_grad, text_grad, head_grad, row_loss.reshape(rows))
 
 

time: 115 us -> 105 us (0.913)
  the two profiles are of different devices: /device:TPU:2 before, /device:TPU:8 now
where the time goes in v3:
time: 105 us; the launch traced here: 104 us
  starting transfers between devices  46.7 us (44%)
  blocking collectives  23.2 us (22%)
  Pallas kernels  16.1 us (15%)
  waiting for transfers between devices  12.2 us (12%)
  local copies, waits for them, and re-layouts  3.51 us (3%)
  between operations  2.1 us (2%)
    ppermute x6, starting transfers between devices, shifted(): lax.ppermute(value, axes, [(i, (i + by) % length) for i in range(length)])  33.4 us
    all_to_all x1, blocking collectives, body(): summed = lax.all_to_all(packed, BLK, 0, 0)  23.2 us
    pallas_call x7, Pallas kernels, kernel_call(): pl.pallas_call(kernel, out_shape=out_shape, in_specs=[pl.BlockSpec(memory...  16.1 us
    ppermute x6, waiting for transfers between devices, shifted(): lax.ppermute(value, axes, [(i, (i + by) % length) for i in range(length)])  9.21 us
    all_to_all x1, starting transfers between devices, body(): met = lax.all_to_all(quads, QUAD, 0, 0)  3.68 us
    unnamed x10, local copies, waits for them, and re-layouts  3.51 us
    all_to_all x1, starting transfers between devices, body(): partial = lax.all_to_all(products, 'x', 0, 0)  3.48 us
    all_to_all x1, waiting for transfers between devices, body(): partial = lax.all_to_all(products, 'x', 0, 0)  2.65 us
  transfers between devices with their start and end apart: 11, of which 5 were waited for; matrix products, arithmetic and copies ran while one was open for 0% of the time, Pallas kernels for 12%

profile of v3, /device:TPU:8, one launch (start us, length us, event | category | flops | bytes accessed | tf_op | source)
XLA Modules:
  0.0 103.9 jit_solution(4962027545661713584)
XLA Ops:
  0.6 2.0 %shard_map.93 = (bf16[136,1152]{1,0:T(8,128)(2,1)}, bf16[136,1152]{1,0:T(8,128)(2,1)}) custom-call(bf16[128,1152]{1,0:T(8,128)(2,1)} %img.2, bf16[128,1152]{1,0:T(8,128)(2,1)} %feats.4, s32[1,128]{1,0:T(1,128)} %bitcast.4), custom_call_target="tpu_custom_call" | custom-call | bytes 1217024 | tf_op jit(solution)/shard_map/pallas_call | solution.py:29
  2.6 17.4 %collective-permute-start.2 = (bf16[136,1152]{1,0:T(8,128)(2,1)}, bf16[136,1152]{1,0:T(8,128)(2,1)S(1)}, u32[]{:S(2)}, u32[]{:S(2)}) collective-permute-start(bf16[136,1152]{1,0:T(8,128)(2,1)} %get-tuple-element.29.img), channel_id=1, source_target_pairs={{0,752},{16,0},{32,16},{48,32},{64,48},{80,64},{96,80},{112,96},{1... | collective-permute-start | bytes 940040 | tf_op jit(solution)/shard_map/ppermute | solution.py:23
  20.0 0.0 copy-start
  20.0 2.1 %collective-permute-start.3 = (bf16[136,1152]{1,0:T(8,128)(2,1)}, bf16[136,1152]{1,0:T(8,128)(2,1)S(1)}, u32[]{:S(2)}, u32[]{:S(2)}) collective-permute-start(bf16[136,1152]{1,0:T(8,128)(2,1)} %get-tuple-element.26.txt), channel_id=1, source_target_pairs={{0,16},{16,32},{32,48},{48,64},{64,80},{80,96},{96,112},{112,128},... | collective-permute-start | bytes 940040 | tf_op jit(solution)/shard_map/ppermute | solution.py:23
  22.1 0.0 copy-start.2
  22.1 1.7 %copy-done.2 = bf16[1152,1152]{1,0:T(8,128)(2,1)S(1)} copy-done((bf16[1152,1152]{1,0:T(8,128)(2,1)S(1)}, bf16[1152,1152]{1,0:T(8,128)(2,1)}, u32[]{:S(2)}) %copy-start.2) | copy-done | bytes 2654232
  23.8 0.0 copy-start.4
  23.8 1.7 %shard_map.94 = (f32[128,1152]{1,0:T(8,128)S(1)}, f32[128,1]{1,0:T(8,128)S(1)}) custom-call(bf16[128,1152]{1,0:T(8,128)(2,1)} %feats.4, bf16[1152,1152]{1,0:T(8,128)(2,1)S(1)} %copy-done.2), custom_call_target="tpu_custom_call" | custom-call | flops 12000000000 | bytes 3539456 | tf_op jit(solution)/shard_map/pallas_call | solution.py:29
  25.6 1.9 %collective-permute-start.4 = (bf16[128,1152]{1,0:T(8,128)(2,1)}, bf16[128,1152]{1,0:T(8,128)(2,1)S(1)}, u32[]{:S(2)}, u32[]{:S(2)}) collective-permute-start(bf16[128,1152]{1,0:T(8,128)(2,1)} %feats.4), channel_id=1, source_target_pairs={{0,1},{1,0},{2,3},{3,2},{4,5},{5,4},{6,7},{7,6},{8,9},{9,8},{10,11... | collective-permute-start | bytes 884744 | tf_op jit(solution)/shard_map/ppermute | solution.py:276
  27.5 0.0 copy-done.4
  27.5 2.4 %collective-permute-start = (bf16[136,1152]{1,0:T(8,128)(2,1)S(1)}, bf16[136,1152]{1,0:T(8,128)(2,1)S(1)}, u32[]{:S(2)}, u32[]{:S(2)}) collective-permute-start(bf16[136,1152]{1,0:T(8,128)(2,1)S(1)} %copy-done.4), channel_id=1, source_target_pairs={{0,1},{1,2},{2,3},{3,4},{4,5},{5,6},{6,7},{7,8},{8,9},{9,10},{10,1... | collective-permute-start | bytes 940040 | tf_op jit(solution)/shard_map/ppermute | solution.py:23
  29.9 0.0 copy-done
  29.9 5.3 %collective-permute-start.1 = (bf16[136,1152]{1,0:T(8,128)(2,1)S(1)}, bf16[136,1152]{1,0:T(8,128)(2,1)S(1)}, u32[]{:S(2)}, u32[]{:S(2)}) collective-permute-start(bf16[136,1152]{1,0:T(8,128)(2,1)S(1)} %copy-done), channel_id=1, source_target_pairs={{0,15},{1,0},{2,1},{3,2},{4,3},{5,4},{6,5},{7,6},{8,7},{9,8},{10,9... | collective-permute-start | bytes 940040 | tf_op jit(solution)/shard_map/ppermute | solution.py:23
  35.2 0.0 collective-permute-done.4.feats_c
  35.2 0.0 collective-permute-done.2.img_b
  35.2 5.4 %collective-permute-done.3.txt_b = bf16[136,1152]{1,0:T(8,128)(2,1)S(1)} collective-permute-done((bf16[136,1152]{1,0:T(8,128)(2,1)}, bf16[136,1152]{1,0:T(8,128)(2,1)S(1)}, u32[]{:S(2)}, u32[]{:S(2)}) %collective-permute-start.3) | collective-permute-done | bytes 313376 | tf_op jit(solution)/shard_map/ppermute | solution.py:23
  40.6 4.0 %collective-permute-start.5 = (bf16[136,1152]{1,0:T(8,128)(2,1)S(1)}, bf16[136,1152]{1,0:T(8,128)(2,1)S(1)}, u32[]{:S(2)}, u32[]{:S(2)}) collective-permute-start(bf16[136,1152]{1,0:T(8,128)(2,1)S(1)} %collective-permute-done.2.img_b), channel_id=1, source_target_pairs={{0,15},{1,0},{2,1},{3,2},{4,3},{5,4},{6,5},{7,6},{8,7},{9,8},{10,9... | collective-permute-start | bytes 940040 | tf_op jit(solution)/shard_map/ppermute | solution.py:23
  44.7 2.2 %collective-permute-start.6 = (bf16[128,1152]{1,0:T(8,128)(2,1)}, bf16[128,1152]{1,0:T(8,128)(2,1)S(1)}, u32[]{:S(2)}, u32[]{:S(2)}) collective-permute-start(bf16[128,1152]{1,0:T(8,128)(2,1)} %feats.4), channel_id=1, source_target_pairs={{0,8},{8,0},{1,9},{9,1},{2,10},{10,2},{3,11},{11,3},{4,12},{12,4},... | collective-permute-start | bytes 884744 | tf_op jit(solution)/shard_map/ppermute | solution.py:279
  48.1 0.0 collective-permute-done.txt_g
  48.2 0.0 collective-permute-done.1.img_g
  48.2 2.3 %collective-permute-done.5.img_bg = bf16[136,1152]{1,0:T(8,128)(2,1)S(1)} collective-permute-done((bf16[136,1152]{1,0:T(8,128)(2,1)S(1)}, bf16[136,1152]{1,0:T(8,128)(2,1)S(1)}, u32[]{:S(2)}, u32[]{:S(2)}) %collective-permute-start.5) | collective-permute-done | bytes 313376 | tf_op jit(solution)/shard_map/ppermute | solution.py:23
  50.4 0.0 copy-start.1
  50.4 2.3 %shard_map.95.turned = bf16[16,72,128]{2,1,0:T(8,128)(2,1)} custom-call(f32[1]{0:T(128)S(6)} %copy.10.scale_log, f32[1]{0:T(128)S(6)} %copy.11.logit_bias, f32[128,1152]{1,0:T(8,128)S(1)} %get-tuple-element.27.unit, f32[128,1]{1,0:T(8,128)S(1)} %get-tuple-element.28.length, bf16[136,1152]{1,0:T(8,128)(2,1)S(1)} %copy-done, ...), custom_call_target="tpu_custom_call" | custom-call | flops 301989888 | bytes 2138624 | tf_op jit(solution)/shard_map/pallas_call | solution.py:29
  52.8 3.7 %all-to-all-start = ((bf16[4,4,72,128]{3,2,1,0:T(8,128)(2,1)}), bf16[4,4,72,128]{3,2,1,0:T(8,128)(2,1)S(1)}, u32[]{:S(2)}, u32[]{:S(2)}) async-start(bf16[4,4,72,128]{3,2,1,0:T(8,128)(2,1)} %bitcast.2), calls=%async_computation | async-start | bytes 589824 | tf_op jit(solution)/shard_map/all_to_all | solution.py:295
  56.4 0.0 collective-permute-done.6.feats_y
  56.4 2.0 %collective-permute-start.7 = (bf16[128,1152]{1,0:T(8,128)(2,1)S(1)}, bf16[128,1152]{1,0:T(8,128)(2,1)S(1)}, u32[]{:S(2)}, u32[]{:S(2)}) collective-permute-start(bf16[128,1152]{1,0:T(8,128)(2,1)S(1)} %collective-permute-done.6.feats_y), channel_id=1, source_target_pairs={{0,1},{1,0},{2,3},{3,2},{4,5},{5,4},{6,7},{7,6},{8,9},{9,8},{10,11... | collective-permute-start | bytes 884744 | tf_op jit(solution)/shard_map/ppermute | solution.py:291
  58.5 2.3 %collective-permute-start.8 = (bf16[136,1152]{1,0:T(8,128)(2,1)S(1)}, bf16[136,1152]{1,0:T(8,128)(2,1)S(1)}, u32[]{:S(2)}, u32[]{:S(2)}) collective-permute-start(bf16[136,1152]{1,0:T(8,128)(2,1)S(1)} %collective-permute-done.3.txt_b), channel_id=1, source_target_pairs={{0,1},{1,2},{2,3},{3,4},{4,5},{5,6},{6,7},{7,8},{8,9},{9,10},{10,1... | collective-permute-start | bytes 940040 | tf_op jit(solution)/shard_map/ppermute | solution.py:23
  60.8 0.0 collective-permute-done.7.feats_cy
  60.8 0.4 all-to-all-done.met
  61.2 2.6 %shard_map.96 = bf16[4,72,1152]{2,1,0:T(8,128)(2,1)} custom-call(s32[1]{0:T(128)} %bitcast.place, bf16[4,4,72,128]{3,2,1,0:T(8,128)(2,1)S(1)} %all-to-all-done.met, bf16[128,1152]{1,0:T(8,128)(2,1)} %feats.4, bf16[128,1152]{1,0:T(8,128)(2,1)S(1)} %collective-permute-done.4.feats_c, bf16[128,1152]{1,0:T(8,128)(2,1)S(1)} %collective-permute-done.6.feats_y, ...), custom_call_target="tpu_custom_call" | custom-call | flops 339738624 | bytes 2138112 | tf_op jit(solution)/shard_map/pallas_call | solution.py:29
  63.8 3.5 %all-to-all-start.1 = ((bf16[4,72,1152]{2,1,0:T(8,128)(2,1)}), bf16[4,72,1152]{2,1,0:T(8,128)(2,1)S(1)}, u32[]{:S(2)}, u32[]{:S(2)}) async-start(bf16[4,72,1152]{2,1,0:T(8,128)(2,1)} %shard_map.96), calls=%async_computation.1 | async-start | bytes 1327104 | tf_op jit(solution)/shard_map/all_to_all | solution.py:303
  67.3 1.6 %collective-permute-done.8.txt_bg = bf16[136,1152]{1,0:T(8,128)(2,1)S(1)} collective-permute-done((bf16[136,1152]{1,0:T(8,128)(2,1)S(1)}, bf16[136,1152]{1,0:T(8,128)(2,1)S(1)}, u32[]{:S(2)}, u32[]{:S(2)}) %collective-permute-start.8) | collective-permute-done | bytes 313376 | tf_op jit(solution)/shard_map/ppermute | solution.py:23
  68.8 0.0 copy-done.1
  68.8 0.0 copy-start.3
  68.8 1.7 %copy-done.3 = bf16[1152,1152]{1,0:T(8,128)(2,1)S(1)} copy-done((bf16[1152,1152]{1,0:T(8,128)(2,1)S(1)}, bf16[1152,1152]{1,0:T(8,128)(2,1)}, u32[]{:S(2)}) %copy-start.3) | copy-done | bytes 2654232
  70.6 6.2 %shard_map.97 = (f32[128,1152]{1,0:T(8,128)}, f32[1,128]{1,0:T(1,128)}, f32[128,1152]{1,0:T(8,128)}) custom-call(f32[1]{0:T(128)S(6)} %copy.10.scale_log, f32[1]{0:T(128)S(6)} %copy.11.logit_bias, bf16[128,1152]{1,0:T(8,128)(2,1)S(1)} %copy-done.1, f32[128,1152]{1,0:T(8,128)S(1)} %get-tuple-element.27.unit, bf16[136,1152]{1,0:T(8,128)(2,1)S(1)} %copy-done.4, ...), custom_call_target="tpu_custom_call" | custom-call | flops 4982833152 | bytes 6267392 | tf_op jit(solution)/shard_map/pallas_call | solution.py:29
  76.8 2.6 %all-to-all-done.1.parts = bf16[4,72,1152]{2,1,0:T(8,128)(2,1)S(1)} async-done(((bf16[4,72,1152]{2,1,0:T(8,128)(2,1)}), bf16[4,72,1152]{2,1,0:T(8,128)(2,1)S(1)}, u32[]{:S(2)}, u32[]{:S(2)}) %all-to-all-start.1) | async-done | bytes 663584 | tf_op jit(solution)/shard_map/all_to_all | solution.py:303
  79.4 0.5 shard_map.98
  79.9 23.2 %all_to_all.15.parts = bf16[48,16,128]{2,1,0:T(8,128)(2,1)S(1)} all-to-all(bf16[48,16,128]{2,1,0:T(8,128)(2,1)S(1)} %shard_map.98), channel_id=1, replica_groups=mesh['yh'=4,'z'=12,'yl'=2,'x'=4,'core'=2] {'yh','z'}, dimensions={0} | all-to-all | bytes 393216 | tf_op jit(solution)/shard_map/all_to_all | solution.py:334
  103.2 0.7 shard_map.99
Async XLA Ops:
  2.6 32.6 %collective-permute-start.2 = (bf16[136,1152]{1,0:T(8,128)(2,1)}, bf16[136,1152]{1,0:T(8,128)(2,1)S(1)}, u32[]{:S(2)}, u32[]{:S(2)}) collective-permute-start(bf16[136,1152]{1,0:T(8,128)(2,1)} %get-tuple-element.29.img), channel_id=1, source_target_pairs={{0,752},{16,0},{32,16},{48,32},{64,48},{80,64},{96,80},{112,96},{1... | collective-permute-start | bytes 940040 | tf_op jit(solution)/shard_map/ppermute | solution.py:23
  20.0 9.9 %copy-start = (bf16[136,1152]{1,0:T(8,128)(2,1)S(1)}, bf16[136,1152]{1,0:T(8,128)(2,1)}, u32[]{:S(2)}) copy-start(bf16[136,1152]{1,0:T(8,128)(2,1)} %get-tuple-element.29.img) | copy-start | bytes 940036
  20.0 20.6 %collective-permute-start.3 = (bf16[136,1152]{1,0:T(8,128)(2,1)}, bf16[136,1152]{1,0:T(8,128)(2,1)S(1)}, u32[]{:S(2)}, u32[]{:S(2)}) collective-permute-start(bf16[136,1152]{1,0:T(8,128)(2,1)} %get-tuple-element.26.txt), channel_id=1, source_target_pairs={{0,16},{16,32},{32,48},{48,64},{64,80},{80,96},{96,112},{112,128},... | collective-permute-start | bytes 940040 | tf_op jit(solution)/shard_map/ppermute | solution.py:23
  22.1 1.8 %copy-start.2 = (bf16[1152,1152]{1,0:T(8,128)(2,1)S(1)}, bf16[1152,1152]{1,0:T(8,128)(2,1)}, u32[]{:S(2)}) copy-start(bf16[1152,1152]{1,0:T(8,128)(2,1)} %head.3) | copy-start | bytes 7962628
  23.8 3.7 %copy-start.4 = (bf16[136,1152]{1,0:T(8,128)(2,1)S(1)}, bf16[136,1152]{1,0:T(8,128)(2,1)}, u32[]{:S(2)}) copy-start(bf16[136,1152]{1,0:T(8,128)(2,1)} %get-tuple-element.26.txt) | copy-start | bytes 940036
  25.6 9.6 %collective-permute-start.4 = (bf16[128,1152]{1,0:T(8,128)(2,1)}, bf16[128,1152]{1,0:T(8,128)(2,1)S(1)}, u32[]{:S(2)}, u32[]{:S(2)}) collective-permute-start(bf16[128,1152]{1,0:T(8,128)(2,1)} %feats.4), channel_id=1, source_target_pairs={{0,1},{1,0},{2,3},{3,2},{4,5},{5,4},{6,7},{7,6},{8,9},{9,8},{10,11... | collective-permute-start | bytes 884744 | tf_op jit(solution)/shard_map/ppermute | solution.py:276
  27.5 20.7 %collective-permute-start = (bf16[136,1152]{1,0:T(8,128)(2,1)S(1)}, bf16[136,1152]{1,0:T(8,128)(2,1)S(1)}, u32[]{:S(2)}, u32[]{:S(2)}) collective-permute-start(bf16[136,1152]{1,0:T(8,128)(2,1)S(1)} %copy-done.4), channel_id=1, source_target_pairs={{0,1},{1,2},{2,3},{3,4},{4,5},{5,6},{6,7},{7,8},{8,9},{9,10},{10,1... | collective-permute-start | bytes 940040 | tf_op jit(solution)/shard_map/ppermute | solution.py:23
  29.9 18.2 %collective-permute-start.1 = (bf16[136,1152]{1,0:T(8,128)(2,1)S(1)}, bf16[136,1152]{1,0:T(8,128)(2,1)S(1)}, u32[]{:S(2)}, u32[]{:S(2)}) collective-permute-start(bf16[136,1152]{1,0:T(8,128)(2,1)S(1)} %copy-done), channel_id=1, source_target_pairs={{0,15},{1,0},{2,1},{3,2},{4,3},{5,4},{6,5},{7,6},{8,7},{9,8},{10,9... | collective-permute-start | bytes 940040 | tf_op jit(solution)/shard_map/ppermute | solution.py:23
  40.6 9.8 %collective-permute-start.5 = (bf16[136,1152]{1,0:T(8,128)(2,1)S(1)}, bf16[136,1152]{1,0:T(8,128)(2,1)S(1)}, u32[]{:S(2)}, u32[]{:S(2)}) collective-permute-start(bf16[136,1152]{1,0:T(8,128)(2,1)S(1)} %collective-permute-done.2.img_b), channel_id=1, source_target_pairs={{0,15},{1,0},{2,1},{3,2},{4,3},{5,4},{6,5},{7,6},{8,7},{9,8},{10,9... | collective-permute-start | bytes 940040 | tf_op jit(solution)/shard_map/ppermute | solution.py:23
  44.7 11.8 %collective-permute-start.6 = (bf16[128,1152]{1,0:T(8,128)(2,1)}, bf16[128,1152]{1,0:T(8,128)(2,1)S(1)}, u32[]{:S(2)}, u32[]{:S(2)}) collective-permute-start(bf16[128,1152]{1,0:T(8,128)(2,1)} %feats.4), channel_id=1, source_target_pairs={{0,8},{8,0},{1,9},{9,1},{2,10},{10,2},{3,11},{11,3},{4,12},{12,4},... | collective-permute-start | bytes 884744 | tf_op jit(solution)/shard_map/ppermute | solution.py:279
  50.4 18.4 %copy-start.1 = (bf16[128,1152]{1,0:T(8,128)(2,1)S(1)}, bf16[128,1152]{1,0:T(8,128)(2,1)}, u32[]{:S(2)}) copy-start(bf16[128,1152]{1,0:T(8,128)(2,1)} %img.2) | copy-start | bytes 884740
  52.8 8.4 %all-to-all-start = ((bf16[4,4,72,128]{3,2,1,0:T(8,128)(2,1)}), bf16[4,4,72,128]{3,2,1,0:T(8,128)(2,1)S(1)}, u32[]{:S(2)}, u32[]{:S(2)}) async-start(bf16[4,4,72,128]{3,2,1,0:T(8,128)(2,1)} %bitcast.2), calls=%async_computation | async-start | bytes 589824 | tf_op jit(solution)/shard_map/all_to_all | solution.py:295
  56.4 4.3 %collective-permute-start.7 = (bf16[128,1152]{1,0:T(8,128)(2,1)S(1)}, bf16[128,1152]{1,0:T(8,128)(2,1)S(1)}, u32[]{:S(2)}, u32[]{:S(2)}) collective-permute-start(bf16[128,1152]{1,0:T(8,128)(2,1)S(1)} %collective-permute-done.6.feats_y), channel_id=1, source_target_pairs={{0,1},{1,0},{2,3},{3,2},{4,5},{5,4},{6,7},{7,6},{8,9},{9,8},{10,11... | collective-permute-start | bytes 884744 | tf_op jit(solution)/shard_map/ppermute | solution.py:291
  58.5 10.3 %collective-permute-start.8 = (bf16[136,1152]{1,0:T(8,128)(2,1)S(1)}, bf16[136,1152]{1,0:T(8,128)(2,1)S(1)}, u32[]{:S(2)}, u32[]{:S(2)}) collective-permute-start(bf16[136,1152]{1,0:T(8,128)(2,1)S(1)} %collective-permute-done.3.txt_b), channel_id=1, source_target_pairs={{0,1},{1,2},{2,3},{3,4},{4,5},{5,6},{6,7},{7,8},{8,9},{9,10},{10,1... | collective-permute-start | bytes 940040 | tf_op jit(solution)/shard_map/ppermute | solution.py:23
  63.8 15.6 %all-to-all-start.1 = ((bf16[4,72,1152]{2,1,0:T(8,128)(2,1)}), bf16[4,72,1152]{2,1,0:T(8,128)(2,1)S(1)}, u32[]{:S(2)}, u32[]{:S(2)}) async-start(bf16[4,72,1152]{2,1,0:T(8,128)(2,1)} %shard_map.96), calls=%async_computation.1 | async-start | bytes 1327104 | tf_op jit(solution)/shard_map/all_to_all | solution.py:303
  68.8 1.8 %copy-start.3 = (bf16[1152,1152]{1,0:T(8,128)(2,1)S(1)}, bf16[1152,1152]{1,0:T(8,128)(2,1)}, u32[]{:S(2)}) copy-start(bf16[1152,1152]{1,0:T(8,128)(2,1)} %head.3) | copy-start | bytes 7962628

commit v4 on v3

--- a/solution.py
+++ b/solution.py
@@ -23,14 +23,17 @@
     return lax.ppermute(value, axes, [(i, (i + by) % length) for i in range(length)])
 
 
-def kernel_call(kernel, out_shape, flops, scalars, arrays, scratch=(), vmem=VMEM_BYTES):
+def kernel_call(
+    kernel, out_shape, flops, scalars, arrays, scratch=(), vmem=VMEM_BYTES, left_out=0
+):
     moved = sum(v.size * v.dtype.itemsize for v in arrays)
     moved += sum(v.size * v.dtype.itemsize for v in jax.tree.leaves(out_shape))
     return pl.pallas_call(
         kernel,
         out_shape=out_shape,
         in_specs=[pl.BlockSpec(memory_space=pltpu.SMEM)] * len(scalars)
-        + [pl.BlockSpec(memory_space=pltpu.VMEM)] * len(arrays),
+        + [pl.BlockSpec(memory_space=pltpu.VMEM)] * (len(arrays) - left_out)
+        + [pl.BlockSpec(memory_space=pl.ANY)] * left_out,
         out_specs=jax.tree.map(lambda _: pl.BlockSpec(memory_space=pltpu.VMEM), out_shape),
         scratch_shapes=scratch,
         compiler_params=pltpu.CompilerParams(vmem_limit_bytes=vmem),
@@ -105,10 +108,16 @@
     return jnp.maximum(value, 0.0) + jnp.log1p(jnp.exp(-jnp.abs(value)))
 
 
-def block_kernel(img, feats, ids, img_block, txt_block):
-    wide = img[...].astype(F32)
+def block_kernel(ids, img, feats, img_block, txt_block, img_buf, txt_buf, arrived):
+    img_copy = pltpu.make_async_copy(img, img_buf, arrived.at[0])
+    txt_copy = pltpu.make_async_copy(feats, txt_buf, arrived.at[1])
+    img_copy.start()
+    txt_copy.start()
+    img_copy.wait()
+    wide = img_buf[...].astype(F32)
     img_block[...] = with_offsets(wide / lengths_of(wide), ids[...])
-    txt_block[...] = with_offsets(feats[...].astype(F32), ids[...])
+    txt_copy.wait()
+    txt_block[...] = with_offsets(txt_buf[...].astype(F32), ids[...])
 
 
 def text_kernel(feats, head, unit, length):
@@ -197,18 +206,24 @@
     text_out[...] = dot_nt(delta, head[...])
 
 
-def head_kernel(place, met, feats, feats_c, feats_y, feats_cy, out):
+def head_kernel(place, met, feats_y, feats_cy, feats, feats_c, out, own_buf, core_buf, arrived):
+    own_copy = pltpu.make_async_copy(feats, own_buf, arrived.at[0])
+    core_copy = pltpu.make_async_copy(feats_c, core_buf, arrived.at[1])
+    own_copy.start()
+    core_copy.start()
     m = place[0]
     across = m + 1 - 2 * lax.rem(m, 2)
-    total = jnp.zeros((met.shape[1] * met.shape[2], feats.shape[1]), F32)
-    for at, block in (
-        (m, feats),
-        (across, feats_c),
-        (lax.rem(m + 2, 4), feats_y),
-        (lax.rem(across + 2, 4), feats_cy),
-    ):
-        columns = met[at].astype(F32).reshape(total.shape[0], met.shape[3]).astype(BF16)
-        total += jnp.dot(columns, block[...], preferred_element_type=F32)
+
+    def product(at, block):
+        columns = met[at].astype(F32).reshape(-1, met.shape[3]).astype(BF16)
+        return jnp.dot(columns, block[...], preferred_element_type=F32)
+
+    total = product(lax.rem(m + 2, 4), feats_y)
+    total += product(lax.rem(across + 2, 4), feats_cy)
+    own_copy.wait()
+    total += product(m, own_buf)
+    core_copy.wait()
+    total += product(across, core_buf)
     out[...] = total.reshape(out.shape).astype(BF16)
 
 
@@ -258,7 +273,18 @@
 
     block = like((rows + 8, width), BF16)
     img, txt = kernel_call(
-        block_kernel, (block, block), 0, (), (image_emb, text_feats, ids), vmem=60 * 1024 * 1024
+        block_kernel,
+        (block, block),
+        0,
+        (),
+        (ids, image_emb, text_feats),
+        (
+            pltpu.VMEM((rows, width), BF16),
+            pltpu.VMEM((rows, width), BF16),
+            pltpu.SemaphoreType.DMA((2,)),
+        ),
+        vmem=60 * 1024 * 1024,
+        left_out=2,
     )
     img_b = shifted(img, BLK, -1)
     txt_b = shifted(txt, BLK, 1)
@@ -298,7 +324,13 @@
         like((N_X, part, width), BF16),
         2 * 4 * rows * width * N_X * part,
         (place,),
-        (met, text_feats, feats_c, feats_y, feats_cy),
+        (met, feats_y, feats_cy, text_feats, feats_c),
+        (
+            pltpu.VMEM((rows, width), BF16),
+            pltpu.VMEM((rows, width), BF16),
+            pltpu.SemaphoreType.DMA((2,)),
+        ),
+        left_out=2,
     )
     partial = lax.all_to_all(products, "x", 0, 0)
     image_grad, row_loss, text_grad = kernel_call(

time: 105 us -> 105 us (level)
  no operation moved by 1% of the time
where the time goes in v4:
time: 105 us; the launch traced here: 104 us
  starting transfers between devices  46.7 us (44%)
  blocking collectives  23.2 us (22%)
  Pallas kernels  16.4 us (16%)
  waiting for transfers between devices  12.2 us (12%)
  local copies, waits for them, and re-layouts  3.51 us (3%)
  between operations  2.12 us (2%)
    ppermute x6, starting transfers between devices, shifted(): lax.ppermute(value, axes, [(i, (i + by) % length) for i in range(length)])  33.4 us
    all_to_all x1, blocking collectives, body(): summed = lax.all_to_all(packed, BLK, 0, 0)  23.2 us
    pallas_call x7, Pallas kernels, kernel_call(): pl.pallas_call(kernel, out_shape=out_shape, in_specs=[pl.BlockSpec(memory...  16.4 us
    ppermute x6, waiting for transfers between devices, shifted(): lax.ppermute(value, axes, [(i, (i + by) % length) for i in range(length)])  9.45 us
    all_to_all x1, starting transfers between devices, body(): met = lax.all_to_all(quads, QUAD, 0, 0)  3.68 us
    unnamed x10, local copies, waits for them, and re-layouts  3.51 us
    all_to_all x1, starting transfers between devices, body(): partial = lax.all_to_all(products, 'x', 0, 0)  3.49 us
    all_to_all x1, waiting for transfers between devices, body(): partial = lax.all_to_all(products, 'x', 0, 0)  2.41 us
  transfers between devices with their start and end apart: 11, of which 5 were waited for; matrix products, arithmetic and copies ran while one was open for 0% of the time, Pallas kernels for 12%

profile of v4, /device:TPU:8, one launch (start us, length us, event | category | flops | bytes accessed | tf_op | source)
XLA Modules:
  0.0 104.3 jit_solution(4487000457506752822)
XLA Ops:
  0.6 2.6 %shard_map.93 = (bf16[136,1152]{1,0:T(8,128)(2,1)}, bf16[136,1152]{1,0:T(8,128)(2,1)}) custom-call(s32[1,128]{1,0:T(1,128)} %bitcast.4, bf16[128,1152]{1,0:T(8,128)(2,1)} %img.2, bf16[128,1152]{1,0:T(8,128)(2,1)} %feats.4), custom_call_target="tpu_custom_call" | custom-call | bytes 1217024 | tf_op jit(solution)/shard_map/pallas_call | solution.py:31
  3.3 17.4 %collective-permute-start.2 = (bf16[136,1152]{1,0:T(8,128)(2,1)}, bf16[136,1152]{1,0:T(8,128)(2,1)S(1)}, u32[]{:S(2)}, u32[]{:S(2)}) collective-permute-start(bf16[136,1152]{1,0:T(8,128)(2,1)} %get-tuple-element.29.img), channel_id=1, source_target_pairs={{0,752},{16,0},{32,16},{48,32},{64,48},{80,64},{96,80},{112,96},{1... | collective-permute-start | bytes 940040 | tf_op jit(solution)/shard_map/ppermute | solution.py:23
  20.6 0.0 copy-start
  20.7 2.1 %collective-permute-start.3 = (bf16[136,1152]{1,0:T(8,128)(2,1)}, bf16[136,1152]{1,0:T(8,128)(2,1)S(1)}, u32[]{:S(2)}, u32[]{:S(2)}) collective-permute-start(bf16[136,1152]{1,0:T(8,128)(2,1)} %get-tuple-element.26.txt), channel_id=1, source_target_pairs={{0,16},{16,32},{32,48},{48,64},{64,80},{80,96},{96,112},{112,128},... | collective-permute-start | bytes 940040 | tf_op jit(solution)/shard_map/ppermute | solution.py:23
  22.7 0.0 copy-start.2
  22.7 1.7 %copy-done.2 = bf16[1152,1152]{1,0:T(8,128)(2,1)S(1)} copy-done((bf16[1152,1152]{1,0:T(8,128)(2,1)S(1)}, bf16[1152,1152]{1,0:T(8,128)(2,1)}, u32[]{:S(2)}) %copy-start.2) | copy-done | bytes 2654232
  24.5 0.0 copy-start.4
  24.5 1.7 %shard_map.94 = (f32[128,1152]{1,0:T(8,128)S(1)}, f32[128,1]{1,0:T(8,128)S(1)}) custom-call(bf16[128,1152]{1,0:T(8,128)(2,1)} %feats.4, bf16[1152,1152]{1,0:T(8,128)(2,1)S(1)} %copy-done.2), custom_call_target="tpu_custom_call" | custom-call | flops 12000000000 | bytes 3539456 | tf_op jit(solution)/shard_map/pallas_call | solution.py:31
  26.2 1.9 %collective-permute-start.4 = (bf16[128,1152]{1,0:T(8,128)(2,1)}, bf16[128,1152]{1,0:T(8,128)(2,1)S(1)}, u32[]{:S(2)}, u32[]{:S(2)}) collective-permute-start(bf16[128,1152]{1,0:T(8,128)(2,1)} %feats.4), channel_id=1, source_target_pairs={{0,1},{1,0},{2,3},{3,2},{4,5},{5,4},{6,7},{7,6},{8,9},{9,8},{10,11... | collective-permute-start | bytes 884744 | tf_op jit(solution)/shard_map/ppermute | solution.py:302
  28.1 0.0 copy-done.4
  28.1 2.4 %collective-permute-start = (bf16[136,1152]{1,0:T(8,128)(2,1)S(1)}, bf16[136,1152]{1,0:T(8,128)(2,1)S(1)}, u32[]{:S(2)}, u32[]{:S(2)}) collective-permute-start(bf16[136,1152]{1,0:T(8,128)(2,1)S(1)} %copy-done.4), channel_id=1, source_target_pairs={{0,1},{1,2},{2,3},{3,4},{4,5},{5,6},{6,7},{7,8},{8,9},{9,10},{10,1... | collective-permute-start | bytes 940040 | tf_op jit(solution)/shard_map/ppermute | solution.py:23
  30.6 0.0 copy-done
  30.6 5.3 %collective-permute-start.1 = (bf16[136,1152]{1,0:T(8,128)(2,1)S(1)}, bf16[136,1152]{1,0:T(8,128)(2,1)S(1)}, u32[]{:S(2)}, u32[]{:S(2)}) collective-permute-start(bf16[136,1152]{1,0:T(8,128)(2,1)S(1)} %copy-done), channel_id=1, source_target_pairs={{0,15},{1,0},{2,1},{3,2},{4,3},{5,4},{6,5},{7,6},{8,7},{9,8},{10,9... | collective-permute-start | bytes 940040 | tf_op jit(solution)/shard_map/ppermute | solution.py:23
  35.8 0.0 collective-permute-done.4.feats_c
  35.9 0.0 collective-permute-done.2.img_b
  35.9 5.4 %collective-permute-done.3.txt_b = bf16[136,1152]{1,0:T(8,128)(2,1)S(1)} collective-permute-done((bf16[136,1152]{1,0:T(8,128)(2,1)}, bf16[136,1152]{1,0:T(8,128)(2,1)S(1)}, u32[]{:S(2)}, u32[]{:S(2)}) %collective-permute-start.3) | collective-permute-done | bytes 313376 | tf_op jit(solution)/shard_map/ppermute | solution.py:23
  41.2 4.0 %collective-permute-start.5 = (bf16[136,1152]{1,0:T(8,128)(2,1)S(1)}, bf16[136,1152]{1,0:T(8,128)(2,1)S(1)}, u32[]{:S(2)}, u32[]{:S(2)}) collective-permute-start(bf16[136,1152]{1,0:T(8,128)(2,1)S(1)} %collective-permute-done.2.img_b), channel_id=1, source_target_pairs={{0,15},{1,0},{2,1},{3,2},{4,3},{5,4},{6,5},{7,6},{8,7},{9,8},{10,9... | collective-permute-start | bytes 940040 | tf_op jit(solution)/shard_map/ppermute | solution.py:23
  45.3 2.2 %collective-permute-start.6 = (bf16[128,1152]{1,0:T(8,128)(2,1)}, bf16[128,1152]{1,0:T(8,128)(2,1)S(1)}, u32[]{:S(2)}, u32[]{:S(2)}) collective-permute-start(bf16[128,1152]{1,0:T(8,128)(2,1)} %feats.4), channel_id=1, source_target_pairs={{0,8},{8,0},{1,9},{9,1},{2,10},{10,2},{3,11},{11,3},{4,12},{12,4},... | collective-permute-start | bytes 884744 | tf_op jit(solution)/shard_map/ppermute | solution.py:305
  48.8 0.0 collective-permute-done.txt_g
  48.8 0.0 collective-permute-done.1.img_g
  48.8 2.3 %collective-permute-done.5.img_bg = bf16[136,1152]{1,0:T(8,128)(2,1)S(1)} collective-permute-done((bf16[136,1152]{1,0:T(8,128)(2,1)S(1)}, bf16[136,1152]{1,0:T(8,128)(2,1)S(1)}, u32[]{:S(2)}, u32[]{:S(2)}) %collective-permute-start.5) | collective-permute-done | bytes 313376 | tf_op jit(solution)/shard_map/ppermute | solution.py:23
  51.1 0.0 copy-start.1
  51.1 2.3 %shard_map.95.turned = bf16[16,72,128]{2,1,0:T(8,128)(2,1)} custom-call(f32[1]{0:T(128)S(6)} %copy.10.scale_log, f32[1]{0:T(128)S(6)} %copy.11.logit_bias, f32[128,1152]{1,0:T(8,128)S(1)} %get-tuple-element.27.unit, f32[128,1]{1,0:T(8,128)S(1)} %get-tuple-element.28.length, bf16[136,1152]{1,0:T(8,128)(2,1)S(1)} %copy-done, ...), custom_call_target="tpu_custom_call" | custom-call | flops 301989888 | bytes 2138624 | tf_op jit(solution)/shard_map/pallas_call | solution.py:31
  53.4 3.7 %all-to-all-start = ((bf16[4,4,72,128]{3,2,1,0:T(8,128)(2,1)}), bf16[4,4,72,128]{3,2,1,0:T(8,128)(2,1)S(1)}, u32[]{:S(2)}, u32[]{:S(2)}) async-start(bf16[4,4,72,128]{3,2,1,0:T(8,128)(2,1)} %bitcast.2), calls=%async_computation | async-start | bytes 589824 | tf_op jit(solution)/shard_map/all_to_all | solution.py:321
  57.1 0.0 collective-permute-done.6.feats_y
  57.1 2.0 %collective-permute-start.7 = (bf16[128,1152]{1,0:T(8,128)(2,1)S(1)}, bf16[128,1152]{1,0:T(8,128)(2,1)S(1)}, u32[]{:S(2)}, u32[]{:S(2)}) collective-permute-start(bf16[128,1152]{1,0:T(8,128)(2,1)S(1)} %collective-permute-done.6.feats_y), channel_id=1, source_target_pairs={{0,1},{1,0},{2,3},{3,2},{4,5},{5,4},{6,7},{7,6},{8,9},{9,8},{10,11... | collective-permute-start | bytes 884744 | tf_op jit(solution)/shard_map/ppermute | solution.py:317
  59.2 2.3 %collective-permute-start.8 = (bf16[136,1152]{1,0:T(8,128)(2,1)S(1)}, bf16[136,1152]{1,0:T(8,128)(2,1)S(1)}, u32[]{:S(2)}, u32[]{:S(2)}) collective-permute-start(bf16[136,1152]{1,0:T(8,128)(2,1)S(1)} %collective-permute-done.3.txt_b), channel_id=1, source_target_pairs={{0,1},{1,2},{2,3},{3,4},{4,5},{5,6},{6,7},{7,8},{8,9},{9,10},{10,1... | collective-permute-start | bytes 940040 | tf_op jit(solution)/shard_map/ppermute | solution.py:23
  61.4 0.0 collective-permute-done.7.feats_cy
  61.4 0.4 all-to-all-done.met
  61.8 2.4 %shard_map.96 = bf16[4,72,1152]{2,1,0:T(8,128)(2,1)} custom-call(s32[1]{0:T(128)} %bitcast.place, bf16[4,4,72,128]{3,2,1,0:T(8,128)(2,1)S(1)} %all-to-all-done.met, bf16[128,1152]{1,0:T(8,128)(2,1)S(1)} %collective-permute-done.6.feats_y, bf16[128,1152]{1,0:T(8,128)(2,1)S(1)} %collective-permute-done.7.feats_cy, bf16[128,1152]{1,0:T(8,128)(2,1)} %feats.4, ...), custom_call_target="tpu_custom_call" | custom-call | flops 339738624 | bytes 2138112 | tf_op jit(solution)/shard_map/pallas_call | solution.py:31
  64.2 3.5 %all-to-all-start.1 = ((bf16[4,72,1152]{2,1,0:T(8,128)(2,1)}), bf16[4,72,1152]{2,1,0:T(8,128)(2,1)S(1)}, u32[]{:S(2)}, u32[]{:S(2)}) async-start(bf16[4,72,1152]{2,1,0:T(8,128)(2,1)} %shard_map.96), calls=%async_computation.1 | async-start | bytes 1327104 | tf_op jit(solution)/shard_map/all_to_all | solution.py:335
  67.7 1.8 %collective-permute-done.8.txt_bg = bf16[136,1152]{1,0:T(8,128)(2,1)S(1)} collective-permute-done((bf16[136,1152]{1,0:T(8,128)(2,1)S(1)}, bf16[136,1152]{1,0:T(8,128)(2,1)S(1)}, u32[]{:S(2)}, u32[]{:S(2)}) %collective-permute-start.8) | collective-permute-done | bytes 313376 | tf_op jit(solution)/shard_map/ppermute | solution.py:23
  69.5 0.0 copy-done.1
  69.5 0.0 copy-start.3
  69.5 1.7 %copy-done.3 = bf16[1152,1152]{1,0:T(8,128)(2,1)S(1)} copy-done((bf16[1152,1152]{1,0:T(8,128)(2,1)S(1)}, bf16[1152,1152]{1,0:T(8,128)(2,1)}, u32[]{:S(2)}) %copy-start.3) | copy-done | bytes 2654232
  71.3 6.2 %shard_map.97 = (f32[128,1152]{1,0:T(8,128)}, f32[1,128]{1,0:T(1,128)}, f32[128,1152]{1,0:T(8,128)}) custom-call(f32[1]{0:T(128)S(6)} %copy.10.scale_log, f32[1]{0:T(128)S(6)} %copy.11.logit_bias, bf16[128,1152]{1,0:T(8,128)(2,1)S(1)} %copy-done.1, f32[128,1152]{1,0:T(8,128)S(1)} %get-tuple-element.27.unit, bf16[136,1152]{1,0:T(8,128)(2,1)S(1)} %copy-done.4, ...), custom_call_target="tpu_custom_call" | custom-call | flops 4982833152 | bytes 6267392 | tf_op jit(solution)/shard_map/pallas_call | solution.py:31
  77.4 2.4 %all-to-all-done.1.parts = bf16[4,72,1152]{2,1,0:T(8,128)(2,1)S(1)} async-done(((bf16[4,72,1152]{2,1,0:T(8,128)(2,1)}), bf16[4,72,1152]{2,1,0:T(8,128)(2,1)S(1)}, u32[]{:S(2)}, u32[]{:S(2)}) %all-to-all-start.1) | async-done | bytes 663584 | tf_op jit(solution)/shard_map/all_to_all | solution.py:335
  79.8 0.5 shard_map.98
  80.3 23.2 %all_to_all.15.parts = bf16[48,16,128]{2,1,0:T(8,128)(2,1)S(1)} all-to-all(bf16[48,16,128]{2,1,0:T(8,128)(2,1)S(1)} %shard_map.98), channel_id=1, replica_groups=mesh['yh'=4,'z'=12,'yl'=2,'x'=4,'core'=2] {'yh','z'}, dimensions={0} | all-to-all | bytes 393216 | tf_op jit(solution)/shard_map/all_to_all | solution.py:366
  103.6 0.7 shard_map.99
Async XLA Ops:
  3.3 32.6 %collective-permute-start.2 = (bf16[136,1152]{1,0:T(8,128)(2,1)}, bf16[136,1152]{1,0:T(8,128)(2,1)S(1)}, u32[]{:S(2)}, u32[]{:S(2)}) collective-permute-start(bf16[136,1152]{1,0:T(8,128)(2,1)} %get-tuple-element.29.img), channel_id=1, source_target_pairs={{0,752},{16,0},{32,16},{48,32},{64,48},{80,64},{96,80},{112,96},{1... | collective-permute-start | bytes 940040 | tf_op jit(solution)/shard_map/ppermute | solution.py:23
  20.6 9.9 %copy-start = (bf16[136,1152]{1,0:T(8,128)(2,1)S(1)}, bf16[136,1152]{1,0:T(8,128)(2,1)}, u32[]{:S(2)}) copy-start(bf16[136,1152]{1,0:T(8,128)(2,1)} %get-tuple-element.29.img) | copy-start | bytes 940036
  20.7 20.6 %collective-permute-start.3 = (bf16[136,1152]{1,0:T(8,128)(2,1)}, bf16[136,1152]{1,0:T(8,128)(2,1)S(1)}, u32[]{:S(2)}, u32[]{:S(2)}) collective-permute-start(bf16[136,1152]{1,0:T(8,128)(2,1)} %get-tuple-element.26.txt), channel_id=1, source_target_pairs={{0,16},{16,32},{32,48},{48,64},{64,80},{80,96},{96,112},{112,128},... | collective-permute-start | bytes 940040 | tf_op jit(solution)/shard_map/ppermute | solution.py:23
  22.7 1.8 %copy-start.2 = (bf16[1152,1152]{1,0:T(8,128)(2,1)S(1)}, bf16[1152,1152]{1,0:T(8,128)(2,1)}, u32[]{:S(2)}) copy-start(bf16[1152,1152]{1,0:T(8,128)(2,1)} %head.3) | copy-start | bytes 7962628
  24.5 3.7 %copy-start.4 = (bf16[136,1152]{1,0:T(8,128)(2,1)S(1)}, bf16[136,1152]{1,0:T(8,128)(2,1)}, u32[]{:S(2)}) copy-start(bf16[136,1152]{1,0:T(8,128)(2,1)} %get-tuple-element.26.txt) | copy-start | bytes 940036
  26.2 9.6 %collective-permute-start.4 = (bf16[128,1152]{1,0:T(8,128)(2,1)}, bf16[128,1152]{1,0:T(8,128)(2,1)S(1)}, u32[]{:S(2)}, u32[]{:S(2)}) collective-permute-start(bf16[128,1152]{1,0:T(8,128)(2,1)} %feats.4), channel_id=1, source_target_pairs={{0,1},{1,0},{2,3},{3,2},{4,5},{5,4},{6,7},{7,6},{8,9},{9,8},{10,11... | collective-permute-start | bytes 884744 | tf_op jit(solution)/shard_map/ppermute | solution.py:302
  28.1 20.7 %collective-permute-start = (bf16[136,1152]{1,0:T(8,128)(2,1)S(1)}, bf16[136,1152]{1,0:T(8,128)(2,1)S(1)}, u32[]{:S(2)}, u32[]{:S(2)}) collective-permute-start(bf16[136,1152]{1,0:T(8,128)(2,1)S(1)} %copy-done.4), channel_id=1, source_target_pairs={{0,1},{1,2},{2,3},{3,4},{4,5},{5,6},{6,7},{7,8},{8,9},{9,10},{10,1... | collective-permute-start | bytes 940040 | tf_op jit(solution)/shard_map/ppermute | solution.py:23
  30.6 18.2 %collective-permute-start.1 = (bf16[136,1152]{1,0:T(8,128)(2,1)S(1)}, bf16[136,1152]{1,0:T(8,128)(2,1)S(1)}, u32[]{:S(2)}, u32[]{:S(2)}) collective-permute-start(bf16[136,1152]{1,0:T(8,128)(2,1)S(1)} %copy-done), channel_id=1, source_target_pairs={{0,15},{1,0},{2,1},{3,2},{4,3},{5,4},{6,5},{7,6},{8,7},{9,8},{10,9... | collective-permute-start | bytes 940040 | tf_op jit(solution)/shard_map/ppermute | solution.py:23
  41.2 9.8 %collective-permute-start.5 = (bf16[136,1152]{1,0:T(8,128)(2,1)S(1)}, bf16[136,1152]{1,0:T(8,128)(2,1)S(1)}, u32[]{:S(2)}, u32[]{:S(2)}) collective-permute-start(bf16[136,1152]{1,0:T(8,128)(2,1)S(1)} %collective-permute-done.2.img_b), channel_id=1, source_target_pairs={{0,15},{1,0},{2,1},{3,2},{4,3},{5,4},{6,5},{7,6},{8,7},{9,8},{10,9... | collective-permute-start | bytes 940040 | tf_op jit(solution)/shard_map/ppermute | solution.py:23
  45.3 11.8 %collective-permute-start.6 = (bf16[128,1152]{1,0:T(8,128)(2,1)}, bf16[128,1152]{1,0:T(8,128)(2,1)S(1)}, u32[]{:S(2)}, u32[]{:S(2)}) collective-permute-start(bf16[128,1152]{1,0:T(8,128)(2,1)} %feats.4), channel_id=1, source_target_pairs={{0,8},{8,0},{1,9},{9,1},{2,10},{10,2},{3,11},{11,3},{4,12},{12,4},... | collective-permute-start | bytes 884744 | tf_op jit(solution)/shard_map/ppermute | solution.py:305
  51.1 18.4 %copy-start.1 = (bf16[128,1152]{1,0:T(8,128)(2,1)S(1)}, bf16[128,1152]{1,0:T(8,128)(2,1)}, u32[]{:S(2)}) copy-start(bf16[128,1152]{1,0:T(8,128)(2,1)} %img.2) | copy-start | bytes 884740
  53.4 8.4 %all-to-all-start = ((bf16[4,4,72,128]{3,2,1,0:T(8,128)(2,1)}), bf16[4,4,72,128]{3,2,1,0:T(8,128)(2,1)S(1)}, u32[]{:S(2)}, u32[]{:S(2)}) async-start(bf16[4,4,72,128]{3,2,1,0:T(8,128)(2,1)} %bitcast.2), calls=%async_computation | async-start | bytes 589824 | tf_op jit(solution)/shard_map/all_to_all | solution.py:321
  57.1 4.3 %collective-permute-start.7 = (bf16[128,1152]{1,0:T(8,128)(2,1)S(1)}, bf16[128,1152]{1,0:T(8,128)(2,1)S(1)}, u32[]{:S(2)}, u32[]{:S(2)}) collective-permute-start(bf16[128,1152]{1,0:T(8,128)(2,1)S(1)} %collective-permute-done.6.feats_y), channel_id=1, source_target_pairs={{0,1},{1,0},{2,3},{3,2},{4,5},{5,4},{6,7},{7,6},{8,9},{9,8},{10,11... | collective-permute-start | bytes 884744 | tf_op jit(solution)/shard_map/ppermute | solution.py:317
  59.2 10.3 %collective-permute-start.8 = (bf16[136,1152]{1,0:T(8,128)(2,1)S(1)}, bf16[136,1152]{1,0:T(8,128)(2,1)S(1)}, u32[]{:S(2)}, u32[]{:S(2)}) collective-permute-start(bf16[136,1152]{1,0:T(8,128)(2,1)S(1)} %collective-permute-done.3.txt_b), channel_id=1, source_target_pairs={{0,1},{1,2},{2,3},{3,4},{4,5},{5,6},{6,7},{7,8},{8,9},{9,10},{10,1... | collective-permute-start | bytes 940040 | tf_op jit(solution)/shard_map/ppermute | solution.py:23
  64.2 15.6 %all-to-all-start.1 = ((bf16[4,72,1152]{2,1,0:T(8,128)(2,1)}), bf16[4,72,1152]{2,1,0:T(8,128)(2,1)S(1)}, u32[]{:S(2)}, u32[]{:S(2)}) async-start(bf16[4,72,1152]{2,1,0:T(8,128)(2,1)} %shard_map.96), calls=%async_computation.1 | async-start | bytes 1327104 | tf_op jit(solution)/shard_map/all_to_all | solution.py:335
  69.5 1.8 %copy-start.3 = (bf16[1152,1152]{1,0:T(8,128)(2,1)S(1)}, bf16[1152,1152]{1,0:T(8,128)(2,1)}, u32[]{:S(2)}) copy-start(bf16[1152,1152]{1,0:T(8,128)(2,1)} %head.3) | copy-start | bytes 7962628

commit v5 on v4

--- a/solution.py
+++ b/solution.py
@@ -108,16 +108,10 @@
     return jnp.maximum(value, 0.0) + jnp.log1p(jnp.exp(-jnp.abs(value)))
 
 
-def block_kernel(ids, img, feats, img_block, txt_block, img_buf, txt_buf, arrived):
-    img_copy = pltpu.make_async_copy(img, img_buf, arrived.at[0])
-    txt_copy = pltpu.make_async_copy(feats, txt_buf, arrived.at[1])
-    img_copy.start()
-    txt_copy.start()
-    img_copy.wait()
-    wide = img_buf[...].astype(F32)
+def block_kernel(img, feats, ids, img_block, txt_block):
+    wide = img[...].astype(F32)
     img_block[...] = with_offsets(wide / lengths_of(wide), ids[...])
-    txt_copy.wait()
-    txt_block[...] = with_offsets(txt_buf[...].astype(F32), ids[...])
+    txt_block[...] = with_offsets(feats[...].astype(F32), ids[...])
 
 
 def text_kernel(feats, head, unit, length):
@@ -273,34 +267,23 @@
 
     block = like((rows + 8, width), BF16)
     img, txt = kernel_call(
-        block_kernel,
-        (block, block),
-        0,
-        (),
-        (ids, image_emb, text_feats),
-        (
-            pltpu.VMEM((rows, width), BF16),
-            pltpu.VMEM((rows, width), BF16),
-            pltpu.SemaphoreType.DMA((2,)),
-        ),
-        vmem=60 * 1024 * 1024,
-        left_out=2,
+        block_kernel, (block, block), 0, (), (image_emb, text_feats, ids), vmem=60 * 1024 * 1024
     )
     img_b = shifted(img, BLK, -1)
     txt_b = shifted(txt, BLK, 1)
     swap = [(0, 1), (1, 0)]
+    feats_c = lax.ppermute(after(text_feats, img), "core", swap)
     unit, length = kernel_call(
         text_kernel,
         (like((rows, width), F32), like((rows, 1), F32)),
         TEXT_FLOPS,
         (),
-        (after(text_feats, img), text_head),
-    )
-    late_img, late_txt, late_feats = lax.optimization_barrier((img, txt, text_feats, unit))[:3]
+        (after(text_feats, feats_c), text_head),
+    )
+    late_img, late_txt = lax.optimization_barrier((img, txt, feats_c))[:2]
     img_g = shifted(late_img, GROUP, -1)
     txt_g = shifted(late_txt, GROUP, 1)
-    feats_c = lax.ppermute(late_feats, "core", swap)
-    img_b, txt_b = lax.optimization_barrier((img_b, txt_b, unit, feats_c))[:2]
+    img_b = after(img_b, unit, feats_c)
     img_bg = shifted(img_b, GROUP, -1)
     feats_y = lax.ppermute(after(text_feats, img_b), "yl", swap)
 
@@ -310,7 +293,7 @@
         like((N_YL * N_CORE * N_X, part, rows), BF16),
         8 * score,
         (scale_log, logit_bias),
-        (after(unit, txt_g), length, img, img_g, img_b, img_bg),
+        (after(unit, txt_b, txt_g), length, img, img_g, img_b, img_bg),
     )
 
     late_b = after(txt_b, turned)

time: 105 us -> 107 us (1.019)
  starting transfers between devices: 46.7 us -> 49 us
  blocking collectives: 23.2 us -> 24.4 us
    all_to_all x1, starting transfers between devices: 3.68 us -> 6.5 us  [body(): met = lax.all_to_all(quads, QUAD, 0, 0)]
    ppermute x6, starting transfers between devices: 33.4 us -> 31.8 us  [shifted(): lax.ppermute(value, axes, [(i, (i + by) % length) for i in range(length)])]
    ppermute x6, waiting for transfers between devices: 9.45 us -> 8.08 us  [shifted(): lax.ppermute(value, axes, [(i, (i + by) % length) for i in range(length)])]
    all_to_all x1, blocking collectives: 23.2 us -> 24.4 us  [body(): summed = lax.all_to_all(packed, BLK, 0, 0)]
where the time goes in v5:
time: 107 us; the launch traced here: 106 us
  starting transfers between devices  49 us (46%)
  blocking collectives  24.4 us (23%)
  Pallas kernels  15.8 us (15%)
  waiting for transfers between devices  11.3 us (11%)
  local copies, waits for them, and re-layouts  3.51 us (3%)
  between operations  2.09 us (2%)
    ppermute x6, starting transfers between devices, shifted(): lax.ppermute(value, axes, [(i, (i + by) % length) for i in range(length)])  31.8 us
    all_to_all x1, blocking collectives, body(): summed = lax.all_to_all(packed, BLK, 0, 0)  24.4 us
    pallas_call x7, Pallas kernels, kernel_call(): pl.pallas_call(kernel, out_shape=out_shape, in_specs=[pl.BlockSpec(memory...  15.8 us
    ppermute x6, waiting for transfers between devices, shifted(): lax.ppermute(value, axes, [(i, (i + by) % length) for i in range(length)])  8.08 us
    all_to_all x1, starting transfers between devices, body(): met = lax.all_to_all(quads, QUAD, 0, 0)  6.5 us
    all_to_all x1, starting transfers between devices, body(): partial = lax.all_to_all(products, 'x', 0, 0)  3.71 us
    unnamed x10, local copies, waits for them, and re-layouts  3.51 us
    ppermute x1, starting transfers between devices, body(): feats_y = lax.ppermute(after(text_feats, img_b), 'yl', swap)  3.04 us
  transfers between devices with their start and end apart: 11, of which 5 were waited for; matrix products, arithmetic and copies ran while one was open for 0% of the time, Pallas kernels for 12%

profile of v5, /device:TPU:8, one launch (start us, length us, event | category | flops | bytes accessed | tf_op | source)
XLA Modules:
  0.0 106.1 jit_solution(7840238766888527826)
XLA Ops:
  0.6 2.0 %shard_map.93 = (bf16[136,1152]{1,0:T(8,128)(2,1)}, bf16[136,1152]{1,0:T(8,128)(2,1)}) custom-call(bf16[128,1152]{1,0:T(8,128)(2,1)} %img.2, bf16[128,1152]{1,0:T(8,128)(2,1)} %feats.4, s32[1,128]{1,0:T(1,128)} %bitcast.4), custom_call_target="tpu_custom_call" | custom-call | bytes 1217024 | tf_op jit(solution)/shard_map/pallas_call | solution.py:31
  2.6 1.9 %collective-permute-start = (bf16[128,1152]{1,0:T(8,128)(2,1)}, bf16[128,1152]{1,0:T(8,128)(2,1)S(1)}, u32[]{:S(2)}, u32[]{:S(2)}) collective-permute-start(bf16[128,1152]{1,0:T(8,128)(2,1)} %feats.4), channel_id=1, source_target_pairs={{0,1},{1,0},{2,3},{3,2},{4,5},{5,4},{6,7},{7,6},{8,9},{9,8},{10,11... | collective-permute-start | bytes 884744 | tf_op jit(solution)/shard_map/ppermute | solution.py:275
  4.5 17.4 %collective-permute-start.4 = (bf16[136,1152]{1,0:T(8,128)(2,1)}, bf16[136,1152]{1,0:T(8,128)(2,1)S(1)}, u32[]{:S(2)}, u32[]{:S(2)}) collective-permute-start(bf16[136,1152]{1,0:T(8,128)(2,1)} %get-tuple-element.29.img), channel_id=1, source_target_pairs={{0,752},{16,0},{32,16},{48,32},{64,48},{80,64},{96,80},{112,96},{1... | collective-permute-start | bytes 940040 | tf_op jit(solution)/shard_map/ppermute | solution.py:23
  21.9 0.0 copy-start
  21.9 2.1 %collective-permute-start.1 = (bf16[136,1152]{1,0:T(8,128)(2,1)}, bf16[136,1152]{1,0:T(8,128)(2,1)S(1)}, u32[]{:S(2)}, u32[]{:S(2)}) collective-permute-start(bf16[136,1152]{1,0:T(8,128)(2,1)} %get-tuple-element.26.txt), channel_id=1, source_target_pairs={{0,16},{16,32},{32,48},{48,64},{64,80},{80,96},{96,112},{112,128},... | collective-permute-start | bytes 940040 | tf_op jit(solution)/shard_map/ppermute | solution.py:23
  24.0 0.0 collective-permute-done.feats_c
  24.0 2.1 %collective-permute-start.2 = (bf16[136,1152]{1,0:T(8,128)(2,1)}, bf16[136,1152]{1,0:T(8,128)(2,1)S(1)}, u32[]{:S(2)}, u32[]{:S(2)}) collective-permute-start(bf16[136,1152]{1,0:T(8,128)(2,1)} %get-tuple-element.26.txt), channel_id=1, source_target_pairs={{0,1},{1,2},{2,3},{3,4},{4,5},{5,6},{6,7},{7,8},{8,9},{9,10},{10,1... | collective-permute-start | bytes 940040 | tf_op jit(solution)/shard_map/ppermute | solution.py:23
  26.1 5.5 %collective-permute-start.3 = (bf16[136,1152]{1,0:T(8,128)(2,1)}, bf16[136,1152]{1,0:T(8,128)(2,1)S(1)}, u32[]{:S(2)}, u32[]{:S(2)}) collective-permute-start(bf16[136,1152]{1,0:T(8,128)(2,1)} %get-tuple-element.29.img), channel_id=1, source_target_pairs={{0,15},{1,0},{2,1},{3,2},{4,3},{5,4},{6,5},{7,6},{8,7},{9,8},{10,9... | collective-permute-start | bytes 940040 | tf_op jit(solution)/shard_map/ppermute | solution.py:23
  31.7 0.0 copy-start.2
  31.7 1.7 %copy-done.2 = bf16[1152,1152]{1,0:T(8,128)(2,1)S(1)} copy-done((bf16[1152,1152]{1,0:T(8,128)(2,1)S(1)}, bf16[1152,1152]{1,0:T(8,128)(2,1)}, u32[]{:S(2)}) %copy-start.2) | copy-done | bytes 2654232
  33.4 1.7 %shard_map.94 = (f32[128,1152]{1,0:T(8,128)S(1)}, f32[128,1]{1,0:T(8,128)S(1)}) custom-call(bf16[128,1152]{1,0:T(8,128)(2,1)} %feats.4, bf16[1152,1152]{1,0:T(8,128)(2,1)S(1)} %copy-done.2), custom_call_target="tpu_custom_call" | custom-call | flops 12000000000 | bytes 3539456 | tf_op jit(solution)/shard_map/pallas_call | solution.py:31
  35.1 0.0 collective-permute-done.4.img_b
  35.1 2.4 %collective-permute-start.5 = (bf16[136,1152]{1,0:T(8,128)(2,1)S(1)}, bf16[136,1152]{1,0:T(8,128)(2,1)S(1)}, u32[]{:S(2)}, u32[]{:S(2)}) collective-permute-start(bf16[136,1152]{1,0:T(8,128)(2,1)S(1)} %collective-permute-done.4.img_b), channel_id=1, source_target_pairs={{0,15},{1,0},{2,1},{3,2},{4,3},{5,4},{6,5},{7,6},{8,7},{9,8},{10,9... | collective-permute-start | bytes 940040 | tf_op jit(solution)/shard_map/ppermute | solution.py:23
  37.6 3.0 %collective-permute-start.6 = (bf16[128,1152]{1,0:T(8,128)(2,1)}, bf16[128,1152]{1,0:T(8,128)(2,1)S(1)}, u32[]{:S(2)}, u32[]{:S(2)}) collective-permute-start(bf16[128,1152]{1,0:T(8,128)(2,1)} %feats.4), channel_id=1, source_target_pairs={{0,8},{8,0},{1,9},{9,1},{2,10},{10,2},{3,11},{11,3},{4,12},{12,4},... | collective-permute-start | bytes 884744 | tf_op jit(solution)/shard_map/ppermute | solution.py:288
  41.9 1.2 %collective-permute-done.1.txt_b = bf16[136,1152]{1,0:T(8,128)(2,1)S(1)} collective-permute-done((bf16[136,1152]{1,0:T(8,128)(2,1)}, bf16[136,1152]{1,0:T(8,128)(2,1)S(1)}, u32[]{:S(2)}, u32[]{:S(2)}) %collective-permute-start.1) | collective-permute-done | bytes 313376 | tf_op jit(solution)/shard_map/ppermute | solution.py:23
  43.1 5.3 %collective-permute-done.2.txt_g = bf16[136,1152]{1,0:T(8,128)(2,1)S(1)} collective-permute-done((bf16[136,1152]{1,0:T(8,128)(2,1)}, bf16[136,1152]{1,0:T(8,128)(2,1)S(1)}, u32[]{:S(2)}, u32[]{:S(2)}) %collective-permute-start.2) | collective-permute-done | bytes 313376 | tf_op jit(solution)/shard_map/ppermute | solution.py:23
  48.4 0.0 collective-permute-done.3.img_g
  48.4 0.0 collective-permute-done.5.img_bg
  48.4 0.0 copy-done
  48.4 0.0 copy-start.1
  48.4 0.0 copy-start.4
  48.5 2.3 %shard_map.95.turned = bf16[16,72,128]{2,1,0:T(8,128)(2,1)} custom-call(f32[1]{0:T(128)S(6)} %copy.10.scale_log, f32[1]{0:T(128)S(6)} %copy.11.logit_bias, f32[128,1152]{1,0:T(8,128)S(1)} %get-tuple-element.27.unit, f32[128,1]{1,0:T(8,128)S(1)} %get-tuple-element.28.length, bf16[136,1152]{1,0:T(8,128)(2,1)S(1)} %copy-done, ...), custom_call_target="tpu_custom_call" | custom-call | flops 301989888 | bytes 2138624 | tf_op jit(solution)/shard_map/pallas_call | solution.py:31
  50.8 6.5 %all-to-all-start = ((bf16[4,4,72,128]{3,2,1,0:T(8,128)(2,1)}), bf16[4,4,72,128]{3,2,1,0:T(8,128)(2,1)S(1)}, u32[]{:S(2)}, u32[]{:S(2)}) async-start(bf16[4,4,72,128]{3,2,1,0:T(8,128)(2,1)} %bitcast.2), calls=%async_computation | async-start | bytes 589824 | tf_op jit(solution)/shard_map/all_to_all | solution.py:304
  57.3 0.0 collective-permute-done.6.feats_y
  57.3 2.0 %collective-permute-start.7 = (bf16[128,1152]{1,0:T(8,128)(2,1)S(1)}, bf16[128,1152]{1,0:T(8,128)(2,1)S(1)}, u32[]{:S(2)}, u32[]{:S(2)}) collective-permute-start(bf16[128,1152]{1,0:T(8,128)(2,1)S(1)} %collective-permute-done.6.feats_y), channel_id=1, source_target_pairs={{0,1},{1,0},{2,3},{3,2},{4,5},{5,4},{6,7},{7,6},{8,9},{9,8},{10,11... | collective-permute-start | bytes 884744 | tf_op jit(solution)/shard_map/ppermute | solution.py:300
  59.4 2.3 %collective-permute-start.8 = (bf16[136,1152]{1,0:T(8,128)(2,1)S(1)}, bf16[136,1152]{1,0:T(8,128)(2,1)S(1)}, u32[]{:S(2)}, u32[]{:S(2)}) collective-permute-start(bf16[136,1152]{1,0:T(8,128)(2,1)S(1)} %collective-permute-done.1.txt_b), channel_id=1, source_target_pairs={{0,1},{1,2},{2,3},{3,4},{4,5},{5,6},{6,7},{7,8},{8,9},{9,10},{10,1... | collective-permute-start | bytes 940040 | tf_op jit(solution)/shard_map/ppermute | solution.py:23
  61.6 0.0 collective-permute-done.7.feats_cy
  61.6 0.4 all-to-all-done.met
  62.0 2.4 %shard_map.96 = bf16[4,72,1152]{2,1,0:T(8,128)(2,1)} custom-call(s32[1]{0:T(128)} %bitcast.place, bf16[4,4,72,128]{3,2,1,0:T(8,128)(2,1)S(1)} %all-to-all-done.met, bf16[128,1152]{1,0:T(8,128)(2,1)S(1)} %collective-permute-done.6.feats_y, bf16[128,1152]{1,0:T(8,128)(2,1)S(1)} %collective-permute-done.7.feats_cy, bf16[128,1152]{1,0:T(8,128)(2,1)} %feats.4, ...), custom_call_target="tpu_custom_call" | custom-call | flops 339738624 | bytes 2138112 | tf_op jit(solution)/shard_map/pallas_call | solution.py:31
  64.4 3.7 %all-to-all-start.1 = ((bf16[4,72,1152]{2,1,0:T(8,128)(2,1)}), bf16[4,72,1152]{2,1,0:T(8,128)(2,1)S(1)}, u32[]{:S(2)}, u32[]{:S(2)}) async-start(bf16[4,72,1152]{2,1,0:T(8,128)(2,1)} %shard_map.96), calls=%async_computation.1 | async-start | bytes 1327104 | tf_op jit(solution)/shard_map/all_to_all | solution.py:318
  68.1 1.6 %collective-permute-done.8.txt_bg = bf16[136,1152]{1,0:T(8,128)(2,1)S(1)} collective-permute-done((bf16[136,1152]{1,0:T(8,128)(2,1)S(1)}, bf16[136,1152]{1,0:T(8,128)(2,1)S(1)}, u32[]{:S(2)}, u32[]{:S(2)}) %collective-permute-start.8) | collective-permute-done | bytes 313376 | tf_op jit(solution)/shard_map/ppermute | solution.py:23
  69.7 0.0 copy-done.1
  69.7 0.0 copy-done.4
  69.7 0.0 copy-start.3
  69.7 1.7 %copy-done.3 = bf16[1152,1152]{1,0:T(8,128)(2,1)S(1)} copy-done((bf16[1152,1152]{1,0:T(8,128)(2,1)S(1)}, bf16[1152,1152]{1,0:T(8,128)(2,1)}, u32[]{:S(2)}) %copy-start.3) | copy-done | bytes 2654232
  71.5 6.2 %shard_map.97 = (f32[128,1152]{1,0:T(8,128)}, f32[1,128]{1,0:T(1,128)}, f32[128,1152]{1,0:T(8,128)}) custom-call(f32[1]{0:T(128)S(6)} %copy.10.scale_log, f32[1]{0:T(128)S(6)} %copy.11.logit_bias, bf16[128,1152]{1,0:T(8,128)(2,1)S(1)} %copy-done.1, f32[128,1152]{1,0:T(8,128)S(1)} %get-tuple-element.27.unit, bf16[136,1152]{1,0:T(8,128)(2,1)S(1)} %copy-done.4, ...), custom_call_target="tpu_custom_call" | custom-call | flops 4982833152 | bytes 6267392 | tf_op jit(solution)/shard_map/pallas_call | solution.py:31
  77.6 2.9 %all-to-all-done.1.parts = bf16[4,72,1152]{2,1,0:T(8,128)(2,1)S(1)} async-done(((bf16[4,72,1152]{2,1,0:T(8,128)(2,1)}), bf16[4,72,1152]{2,1,0:T(8,128)(2,1)S(1)}, u32[]{:S(2)}, u32[]{:S(2)}) %all-to-all-start.1) | async-done | bytes 663584 | tf_op jit(solution)/shard_map/all_to_all | solution.py:318
  80.5 0.5 shard_map.98
  81.0 24.4 %all_to_all.15.parts = bf16[48,16,128]{2,1,0:T(8,128)(2,1)S(1)} all-to-all(bf16[48,16,128]{2,1,0:T(8,128)(2,1)S(1)} %shard_map.98), channel_id=1, replica_groups=mesh['yh'=4,'z'=12,'yl'=2,'x'=4,'core'=2] {'yh','z'}, dimensions={0} | all-to-all | bytes 393216 | tf_op jit(solution)/shard_map/all_to_all | solution.py:349
  105.4 0.7 shard_map.99
Async XLA Ops:
  2.6 21.4 %collective-permute-start = (bf16[128,1152]{1,0:T(8,128)(2,1)}, bf16[128,1152]{1,0:T(8,128)(2,1)S(1)}, u32[]{:S(2)}, u32[]{:S(2)}) collective-permute-start(bf16[128,1152]{1,0:T(8,128)(2,1)} %feats.4), channel_id=1, source_target_pairs={{0,1},{1,0},{2,3},{3,2},{4,5},{5,4},{6,7},{7,6},{8,9},{9,8},{10,11... | collective-permute-start | bytes 884744 | tf_op jit(solution)/shard_map/ppermute | solution.py:275
  4.5 30.6 %collective-permute-start.4 = (bf16[136,1152]{1,0:T(8,128)(2,1)}, bf16[136,1152]{1,0:T(8,128)(2,1)S(1)}, u32[]{:S(2)}, u32[]{:S(2)}) collective-permute-start(bf16[136,1152]{1,0:T(8,128)(2,1)} %get-tuple-element.29.img), channel_id=1, source_target_pairs={{0,752},{16,0},{32,16},{48,32},{64,48},{80,64},{96,80},{112,96},{1... | collective-permute-start | bytes 940040 | tf_op jit(solution)/shard_map/ppermute | solution.py:23
  21.9 26.5 %copy-start = (bf16[136,1152]{1,0:T(8,128)(2,1)S(1)}, bf16[136,1152]{1,0:T(8,128)(2,1)}, u32[]{:S(2)}) copy-start(bf16[136,1152]{1,0:T(8,128)(2,1)} %get-tuple-element.29.img) | copy-start | bytes 940036
  21.9 21.2 %collective-permute-start.1 = (bf16[136,1152]{1,0:T(8,128)(2,1)}, bf16[136,1152]{1,0:T(8,128)(2,1)S(1)}, u32[]{:S(2)}, u32[]{:S(2)}) collective-permute-start(bf16[136,1152]{1,0:T(8,128)(2,1)} %get-tuple-element.26.txt), channel_id=1, source_target_pairs={{0,16},{16,32},{32,48},{48,64},{64,80},{80,96},{96,112},{112,128},... | collective-permute-start | bytes 940040 | tf_op jit(solution)/shard_map/ppermute | solution.py:23
  24.0 24.4 %collective-permute-start.2 = (bf16[136,1152]{1,0:T(8,128)(2,1)}, bf16[136,1152]{1,0:T(8,128)(2,1)S(1)}, u32[]{:S(2)}, u32[]{:S(2)}) collective-permute-start(bf16[136,1152]{1,0:T(8,128)(2,1)} %get-tuple-element.26.txt), channel_id=1, source_target_pairs={{0,1},{1,2},{2,3},{3,4},{4,5},{5,6},{6,7},{7,8},{8,9},{9,10},{10,1... | collective-permute-start | bytes 940040 | tf_op jit(solution)/shard_map/ppermute | solution.py:23
  26.1 22.3 %collective-permute-start.3 = (bf16[136,1152]{1,0:T(8,128)(2,1)}, bf16[136,1152]{1,0:T(8,128)(2,1)S(1)}, u32[]{:S(2)}, u32[]{:S(2)}) collective-permute-start(bf16[136,1152]{1,0:T(8,128)(2,1)} %get-tuple-element.29.img), channel_id=1, source_target_pairs={{0,15},{1,0},{2,1},{3,2},{4,3},{5,4},{6,5},{7,6},{8,7},{9,8},{10,9... | collective-permute-start | bytes 940040 | tf_op jit(solution)/shard_map/ppermute | solution.py:23
  31.7 1.8 %copy-start.2 = (bf16[1152,1152]{1,0:T(8,128)(2,1)S(1)}, bf16[1152,1152]{1,0:T(8,128)(2,1)}, u32[]{:S(2)}) copy-start(bf16[1152,1152]{1,0:T(8,128)(2,1)} %head.3) | copy-start | bytes 7962628
  35.1 13.3 %collective-permute-start.5 = (bf16[136,1152]{1,0:T(8,128)(2,1)S(1)}, bf16[136,1152]{1,0:T(8,128)(2,1)S(1)}, u32[]{:S(2)}, u32[]{:S(2)}) collective-permute-start(bf16[136,1152]{1,0:T(8,128)(2,1)S(1)} %collective-permute-done.4.img_b), channel_id=1, source_target_pairs={{0,15},{1,0},{2,1},{3,2},{4,3},{5,4},{6,5},{7,6},{8,7},{9,8},{10,9... | collective-permute-start | bytes 940040 | tf_op jit(solution)/shard_map/ppermute | solution.py:23
  37.6 19.7 %collective-permute-start.6 = (bf16[128,1152]{1,0:T(8,128)(2,1)}, bf16[128,1152]{1,0:T(8,128)(2,1)S(1)}, u32[]{:S(2)}, u32[]{:S(2)}) collective-permute-start(bf16[128,1152]{1,0:T(8,128)(2,1)} %feats.4), channel_id=1, source_target_pairs={{0,8},{8,0},{1,9},{9,1},{2,10},{10,2},{3,11},{11,3},{4,12},{12,4},... | collective-permute-start | bytes 884744 | tf_op jit(solution)/shard_map/ppermute | solution.py:288
  48.4 21.3 %copy-start.1 = (bf16[128,1152]{1,0:T(8,128)(2,1)S(1)}, bf16[128,1152]{1,0:T(8,128)(2,1)}, u32[]{:S(2)}) copy-start(bf16[128,1152]{1,0:T(8,128)(2,1)} %img.2) | copy-start | bytes 884740
  48.4 21.3 %copy-start.4 = (bf16[136,1152]{1,0:T(8,128)(2,1)S(1)}, bf16[136,1152]{1,0:T(8,128)(2,1)}, u32[]{:S(2)}) copy-start(bf16[136,1152]{1,0:T(8,128)(2,1)} %get-tuple-element.26.txt) | copy-start | bytes 940036
  50.8 11.2 %all-to-all-start = ((bf16[4,4,72,128]{3,2,1,0:T(8,128)(2,1)}), bf16[4,4,72,128]{3,2,1,0:T(8,128)(2,1)S(1)}, u32[]{:S(2)}, u32[]{:S(2)}) async-start(bf16[4,4,72,128]{3,2,1,0:T(8,128)(2,1)} %bitcast.2), calls=%async_computation | async-start | bytes 589824 | tf_op jit(solution)/shard_map/all_to_all | solution.py:304
  57.3 4.3 %collective-permute-start.7 = (bf16[128,1152]{1,0:T(8,128)(2,1)S(1)}, bf16[128,1152]{1,0:T(8,128)(2,1)S(1)}, u32[]{:S(2)}, u32[]{:S(2)}) collective-permute-start(bf16[128,1152]{1,0:T(8,128)(2,1)S(1)} %collective-permute-done.6.feats_y), channel_id=1, source_target_pairs={{0,1},{1,0},{2,3},{3,2},{4,5},{5,4},{6,7},{7,6},{8,9},{9,8},{10,11... | collective-permute-start | bytes 884744 | tf_op jit(solution)/shard_map/ppermute | solution.py:300
  59.4 10.3 %collective-permute-start.8 = (bf16[136,1152]{1,0:T(8,128)(2,1)S(1)}, bf16[136,1152]{1,0:T(8,128)(2,1)S(1)}, u32[]{:S(2)}, u32[]{:S(2)}) collective-permute-start(bf16[136,1152]{1,0:T(8,128)(2,1)S(1)} %collective-permute-done.1.txt_b), channel_id=1, source_target_pairs={{0,1},{1,2},{2,3},{3,4},{4,5},{5,6},{6,7},{7,8},{8,9},{9,10},{10,1... | collective-permute-start | bytes 940040 | tf_op jit(solution)/shard_map/ppermute | solution.py:23
  64.4 16.1 %all-to-all-start.1 = ((bf16[4,72,1152]{2,1,0:T(8,128)(2,1)}), bf16[4,72,1152]{2,1,0:T(8,128)(2,1)S(1)}, u32[]{:S(2)}, u32[]{:S(2)}) async-start(bf16[4,72,1152]{2,1,0:T(8,128)(2,1)} %shard_map.96), calls=%async_computation.1 | async-start | bytes 1327104 | tf_op jit(solution)/shard_map/all_to_all | solution.py:318
  69.7 1.8 %copy-start.3 = (bf16[1152,1152]{1,0:T(8,128)(2,1)S(1)}, bf16[1152,1152]{1,0:T(8,128)(2,1)}, u32[]{:S(2)}) copy-start(bf16[1152,1152]{1,0:T(8,128)(2,1)} %head.3) | copy-start | bytes 7962628
